TPU v7x, 512 devices: a whole 4x8x8 slice. The times are simulated.
512 devices in a mesh: lat: 32 (over x_hi, y, core), lon: 16 (over x_lo, z).
Axes of the slice: x: 4 (x_hi: 2, x_lo: 2; x = x_hi * 2 + x_lo), y: 8, z: 8, core: 2. Of those that a mesh axis runs over, the one named last changes fastest.
Arguments:
- level_fields: float32 [2, 2, 640, 2560], P(None, None, 'lat', 'lon'), may hold values from -6 to 6
- wind_field: float32 [2, 2, 640, 2560], P(None, None, 'lat', 'lon'), may hold values from -6 to 6
- zonal_step: float32 [640], P('lat'), may hold values from 0.1 to 1
- quad_weight: float32 [640], P('lat'), may hold values from 0.005 to 0.05
- legendre: bfloat16 [640, 640, 640], P('lon', 'lat'), may hold values from -6 to 6
- wave_table: int32 [640], replicated, may hold values from 0 to 639, as said below
- damping: float32 [2], replicated, may hold values from 0.5 to 20
- vertical: float32 [2, 2], replicated, may hold values from -4 to 4
Outputs:
- new_fields: float32 [2, 2, 640, 2560], P(None, None, 'lat', 'lon')
- spectrum: float32 [640, 640, 2, 2], P('lat', 'lon')
Inputs may be any that keep to these rules, and one draw needn't show every extreme that they name: `wave_table`: slots 2k and 2k+1 hold wavenumbers p and 639 - p; every wavenumber appears in exactly one slot.
All inputs are finite; a program needn't handle non-finite values.
Results may differ from a plain program's by a relative error of at most 0.0038.
Values may be sent and summed in bfloat16 or wider, within the bound.
A program may use at most 64 MiB of HBM per device.

v0:
```python
import math

import jax
import jax.numpy as jnp
from jax import lax
from jax.sharding import PartitionSpec as P

NLON = 2560
M = 640


HIGHEST_PRECISION = lax.Precision.HIGHEST


def padded(cells, sides, width):
    for axis, dim in sides:
        count = lax.axis_size(axis)
        head = lax.slice_in_dim(cells, 0, width, axis=dim)
        tail = lax.slice_in_dim(cells, cells.shape[dim] - width, cells.shape[dim], axis=dim)
        cells = jnp.concatenate(
            [
                lax.ppermute(tail, axis, [(i, (i + 1) % count) for i in range(count)]),
                cells,
                lax.ppermute(head, axis, [((i + 1) % count, i) for i in range(count)]),
            ],
            axis=dim,
        )
    return cells


def angle_table(waves, columns):
    return (waves[:, None] * columns[None, :] % NLON).astype(jnp.float32) * (2.0 * math.pi / NLON)


def correct(spectrum, degrees, damping, vertical):
    modal = jnp.einsum("kl,nmcl->nmck", vertical, spectrum, precision=HIGHEST_PRECISION)
    divisor = 1.0 + damping[None, :] * (degrees * (degrees + 1)).astype(jnp.float32)[
        :, None
    ] / float(M * M)
    modal = modal / divisor[:, None, None, :]
    return jnp.einsum("kl,nmck->nmcl", vertical, modal, precision=HIGHEST_PRECISION)


def shards(
    level_fields, wind_field, zonal_step, quad_weight, legendre, wave_table, damping, vertical
):
    levels, hemis, rows_half, lon_dev = level_fields.shape
    slots_dev = legendre.shape[0]
    lat_count = lax.axis_size("lat")
    lat_index = lax.axis_index("lat")
    lon_index = lax.axis_index("lon")
    degree_dev = M // lat_count
    grid_count = levels * hemis * rows_half
    contract_last = (((1,), (1,)), ((), ()))
    contract_first = (((0,), (0,)), ((), ()))
    batch_slots = (((2,), (1,)), ((0,), (0,)))
    extended = padded(level_fields, (("lat", 2), ("lon", 3)), 1)
    eastward = extended[:, :, 1:-1, 2:]
    westward = extended[:, :, 1:-1, :-2]
    toward = extended[:, :, 2:, 1:-1]
    poleward = extended[:, :, :-2, 1:-1]
    row_number = jnp.arange(rows_half)
    at_equator = (row_number == rows_half - 1) & (lat_index == lat_count - 1)
    toward = jnp.where(at_equator[:, None], level_fields[:, ::-1, -1:, :], toward)
    at_pole = (row_number == 0) & (lat_index == 0)
    poleward = jnp.where(at_pole[:, None], 0.0, poleward)
    tendency = wind_field[0] * zonal_step[:, None] * (eastward - westward) + 0.25 * wind_field[
        1
    ] * (toward - poleward)
    stepped = level_fields - tendency
    my_waves = lax.dynamic_slice_in_dim(wave_table, lon_index * slots_dev, slots_dev)
    portion = lax.all_gather(stepped, "lon", axis=3, tiled=True)
    lon_width = portion.shape[3]
    columns = jnp.arange(lon_width, dtype=jnp.int32)
    angles = angle_table(my_waves, columns)
    values = portion.reshape(grid_count, lon_width)
    cosine_sum = lax.dot_general(
        jnp.cos(angles), values, contract_last, precision=HIGHEST_PRECISION
    )
    sine_sum = lax.dot_general(jnp.sin(angles), values, contract_last, precision=HIGHEST_PRECISION)
    cosine_sum, sine_sum = (cosine_sum, sine_sum)
    fourier = jnp.stack([cosine_sum, -sine_sum], axis=1) / math.sqrt(NLON)
    weighted = (fourier.reshape(slots_dev, 2, levels, hemis, rows_half) * quad_weight).astype(
        jnp.bfloat16
    )
    weighted = weighted.reshape(slots_dev, 2 * levels * hemis, rows_half)
    table_part = legendre
    summed = lax.dot_general(weighted, table_part, batch_slots, preferred_element_type=jnp.float32)
    summed = summed.reshape(slots_dev, 2, levels, hemis, degree_dev * lax.axis_size("lat"))
    degrees = jnp.arange(degree_dev * lax.axis_size("lat"), dtype=jnp.int32)
    parity = jnp.where((degrees[None, :] - my_waves[:, None]) % 2 == 0, 1.0, -1.0)
    kept_mask = degrees[None, :] >= my_waves[:, None]
    combined = summed[:, :, :, 0] + parity[:, None, None, :] * summed[:, :, :, 1]
    combined = jnp.where(kept_mask[:, None, None, :], combined, 0.0)
    raw = lax.psum_scatter(combined.transpose(3, 0, 1, 2), "lat", scatter_dimension=0, tiled=True)
    my_degrees = lat_index * degree_dev + jnp.arange(degree_dev, dtype=jnp.int32)
    spectrum = correct(raw, my_degrees, damping, vertical)
    portion = lax.all_gather(spectrum.astype(jnp.bfloat16), "lat", axis=0, tiled=True)
    row_count = portion.shape[0]
    table_part = legendre
    degrees = jnp.arange(row_count, dtype=jnp.int32)
    even_mask = ((degrees[None, :] - my_waves[:, None]) % 2 == 0)[:, :, None]
    arranged = portion.transpose(1, 0, 2, 3).reshape(slots_dev, row_count, 2 * levels)
    even_sum = lax.dot_general(
        table_part,
        jnp.where(even_mask, arranged, 0),
        batch_slots,
        preferred_element_type=jnp.float32,
    )
    odd_sum = lax.dot_general(
        table_part,
        jnp.where(even_mask, 0, arranged),
        batch_slots,
        preferred_element_type=jnp.float32,
    )
    even_sum, odd_sum = (even_sum, odd_sum)
    coefs = jnp.stack([even_sum + odd_sum, even_sum - odd_sum], axis=1) / math.sqrt(M)
    coefs = (
        coefs.reshape(slots_dev, 2, rows_half, 2, levels)
        .transpose(0, 3, 4, 1, 2)
        .reshape(slots_dev, 2, grid_count)
    )
    my_columns = lon_index * lon_dev + jnp.arange(lon_dev, dtype=jnp.int32)
    portion = lax.all_gather(coefs, "lon", axis=0, tiled=True)
    factor = jnp.where(wave_table == 0, 1.0, 2.0)[:, None]
    angles = angle_table(wave_table, my_columns)
    totals = lax.dot_general(
        portion[:, 0], jnp.cos(angles) * factor, contract_first, precision=HIGHEST_PRECISION
    )
    grid_out = totals - lax.dot_general(
        portion[:, 1], jnp.sin(angles) * factor, contract_first, precision=HIGHEST_PRECISION
    )
    new_fields = (grid_out / math.sqrt(NLON)).reshape(level_fields.shape)
    return (new_fields, spectrum)


def solution(mesh):
    return jax.shard_map(
        shards,
        mesh=mesh,
        in_specs=(
            P(None, None, "lat", "lon"),
            P(None, None, "lat", "lon"),
            P("lat"),
            P("lat"),
            P("lon", "lat", None),
            P(),
            P(),
            P(),
        ),
        out_specs=(P(None, None, "lat", "lon"), P("lat", "lon", None, None)),
        check_vma=False,
    )
```

profile of v0, /device:TPU:1, one launch (start us, length us, event | category | flops | bytes accessed | tf_op | source)
XLA Modules:
  0.0 499.0 jit_solution(7811665104640846903)
XLA Ops:
  7.2 0.8 fusion.88
  8.0 4.6 collective-permute-start
  12.6 6.1 %collective-permute-start.1 = (f32[2,2,1,160]{3,1,2,0:T(2,128)S(1)}, f32[2,2,1,160]{3,1,2,0:T(2,128)S(1)}, u32[]{:S(2)}, u32[]{:S(2)}) collective-permute-start(f32[2,2,1,160]{3,1,2,0:T(2,128)S(1)} %get-tuple-element.29), channel_id=1, source_target_pairs={{16,0},{32,16},{48,32},{64,48},{80,64},{96,80},{112,96},{128,112},... | collective-permute-start | bytes 7688 | tf_op jit(solution)/shard_map/ppermute | solution.py:24
  18.7 0.8 dynamic_slice.3
  19.5 0.9 fusion.33
  20.6 0.7 broadcast_multiply_fusion
  21.2 0.9 multiply_bitcast_fusion.1
  22.2 1.1 copy.133
  23.9 7.4 %collective-permute-start.2 = (f32[2,2,22,1]{3,1,2,0:T(2,128)S(1)}, f32[2,2,22,1]{3,1,2,0:T(2,128)S(1)}, u32[]{:S(2)}, u32[]{:S(2)}) collective-permute-start(f32[2,2,22,1]{3,1,2,0:T(2,128)S(1)} %get-tuple-element.23), channel_id=1, source_target_pairs={{1,0},{2,1},{3,2},{4,3},{5,4},{6,5},{7,6},{8,7},{9,8},{10,9},{11,1... | collective-permute-start | bytes 1064 | tf_op jit(solution)/shard_map/ppermute | solution.py:24
  31.4 1.9 collective-permute-start.3
  34.0 4.3 collective-permute-done.3
  38.3 0.9 pad_maximum_fusion.3
  39.4 1.1 copy.156
  40.6 0.6 add_subtract_fusion
  41.2 70.2 %all_gather.9 = f32[2,2,20,2560]{2,1,0,3:T(2,128)} all-gather(f32[2,2,20,160]{2,1,0,3:T(2,128)S(1)} %add_subtract_fusion), channel_id=1, replica_groups=mesh['lat'=32,'lon'=16] {'lon'}, dimensions={3}, use_global_device_ids=true | all-gather | bytes 870400 | tf_op jit(solution)/shard_map/all_gather | solution.py:72
  111.4 5.7 %copy.134 = f32[2,2,20,2560]{3,2,1,0:T(8,128)S(1)} copy(f32[2,2,20,2560]{2,1,0,3:T(2,128)} %all_gather.9) | data formatting | bytes 1638400 | tf_op jit(solution)/shard_map/all_gather | solution.py:72
  117.2 2.5 convolution_bitcast_fusion
  119.7 2.4 convolution_negate_fusion
  123.2 0.6 fusion.84
  123.8 1.6 copy.159
  125.4 2.2 copy.160
  127.6 4.0 fusion.2
  132.7 1.3 dynamic-slice
  134.7 275.5 %all-reduce.3.cloned.1.call-done = f32[640,40,2,2]{1,3,2,0:T(2,128)} async-done(((f32[640,40,2,2]{1,3,2,0:T(2,128)}), f32[640,40,2,2]{1,3,2,0:T(2,128)}) %all-reduce.3.cloned.1.call-update) | async-done | bytes 409616
  410.2 1.1 convolution_divide_fusion
  411.2 1.0 fusion.89
  412.2 39.7 %all_gather.10 = bf16[640,40,2,2]{1,3,2,0:T(2,128)(2,1)S(1)} all-gather(bf16[20,40,2,2]{1,3,2,0:T(2,128)(2,1)S(1)} %get-tuple-element.33), channel_id=1, replica_groups=mesh['lat'=32,'lon'=16] {'lat'}, dimensions={0}, use_global_device_ids=true | all-gather | bytes 211200 | tf_op jit(solution)/shard_map/all_gather | solution.py:98
  451.9 0.8 copy.143
  454.1 30.4 %all_gather.11 = f32[640,2,80]{2,1,0:T(2,128)S(1)} all-gather(f32[40,2,80]{2,1,0:T(2,128)S(1)} %copy.149), channel_id=1, replica_groups=mesh['lat'=32,'lon'=16] {'lon'}, dimensions={0}, use_global_device_ids=true | all-gather | bytes 435200 | tf_op jit(solution)/shard_map/all_gather | solution.py:124
  485.0 3.2 fusion.14
  488.2 3.2 fusion.9
  491.5 0.7 copy.150
  (53 shorter events, 5.9 us)
Async XLA Ops:
  7.2 115.2 %copy-start = (bf16[40,20,640]{2,0,1:T(8,128)(2,1)S(1)}, bf16[40,20,640]{2,0,1:T(8,128)(2,1)}, u32[]{:S(2)}) copy-start(bf16[40,20,640]{2,0,1:T(8,128)(2,1)} %param.12) | copy-start | bytes 3072004
  7.2 16.6 %copy-start.1 = (f32[2,2,20,160]{3,1,2,0:T(2,128)S(1)}, f32[2,2,20,160]{3,1,2,0:T(2,128)}, u32[]{:S(2)}) copy-start(f32[2,2,20,160]{3,1,2,0:T(2,128)} %param.8) | copy-start | bytes 153604
  7.2 403.0 %all-reduce.3.cloned.1.call-start = ((), (), s32[]{:S(2)}) async-start(), calls=%async_computation | async-start | bytes 2621440
  8.0 15.7 %collective-permute-start = (f32[2,2,1,160]{3,1,2,0:T(2,128)S(1)}, f32[2,2,1,160]{3,1,2,0:T(2,128)S(1)}, u32[]{:S(2)}, u32[]{:S(2)}) collective-permute-start(f32[2,2,1,160]{3,1,2,0:T(2,128)S(1)} %get-tuple-element.30), channel_id=1, source_target_pairs={{0,16},{16,32},{32,48},{48,64},{64,80},{80,96},{96,112},{112,128},... | collective-permute-start | bytes 7688 | tf_op jit(solution)/shard_map/ppermute | solution.py:22
  12.6 11.1 %collective-permute-start.1 = (f32[2,2,1,160]{3,1,2,0:T(2,128)S(1)}, f32[2,2,1,160]{3,1,2,0:T(2,128)S(1)}, u32[]{:S(2)}, u32[]{:S(2)}) collective-permute-start(f32[2,2,1,160]{3,1,2,0:T(2,128)S(1)} %get-tuple-element.29), channel_id=1, source_target_pairs={{16,0},{32,16},{48,32},{64,48},{80,64},{96,80},{112,96},{128,112},... | collective-permute-start | bytes 7688 | tf_op jit(solution)/shard_map/ppermute | solution.py:24
  23.9 10.0 %collective-permute-start.2 = (f32[2,2,22,1]{3,1,2,0:T(2,128)S(1)}, f32[2,2,22,1]{3,1,2,0:T(2,128)S(1)}, u32[]{:S(2)}, u32[]{:S(2)}) collective-permute-start(f32[2,2,22,1]{3,1,2,0:T(2,128)S(1)} %get-tuple-element.23), channel_id=1, source_target_pairs={{1,0},{2,1},{3,2},{4,3},{5,4},{6,5},{7,6},{8,7},{9,8},{10,9},{11,1... | collective-permute-start | bytes 1064 | tf_op jit(solution)/shard_map/ppermute | solution.py:24
  31.4 6.9 %collective-permute-start.3 = (f32[2,2,22,1]{3,1,2,0:T(2,128)S(1)}, f32[2,2,22,1]{3,1,2,0:T(2,128)S(1)}, u32[]{:S(2)}, u32[]{:S(2)}) collective-permute-start(f32[2,2,22,1]{3,1,2,0:T(2,128)S(1)} %get-tuple-element.22), channel_id=1, source_target_pairs={{0,1},{1,2},{2,3},{3,4},{4,5},{5,6},{6,7},{7,8},{8,9},{9,10},{10,1... | collective-permute-start | bytes 1064 | tf_op jit(solution)/shard_map/ppermute | solution.py:22
  125.4 2.3 copy-start.3
  131.6 0.7 copy-start.5
  131.6 0.9 copy-start.2
  131.6 3.0 copy-start.4
  131.6 278.5 %copy-start.6 = (f32[2,2]{1,0:T(2,128)S(1)}, f32[2,2]{1,0:T(2,128)}, u32[]{:S(2)}) copy-start(f32[2,2]{1,0:T(2,128)} %param.15) | copy-start | bytes 52
Sparse Core Ops, SparseCore 0:
  131.8 278.3 all-reduce.2
where the time goes:
time: 505 us; the launch traced here: 499 us
  waiting for transfers between devices  280 us (55%)
  blocking collectives  140 us (28%)
  local copies, waits for them, and re-layouts  20.7 us (4%)
  starting transfers between devices  20.1 us (4%)
  between operations  15.1 us (3%)
  matrix products  14.6 us (3%)
  other arithmetic  8.39 us (2%)
    unnamed x2, waiting for transfers between devices  276 us
    all_gather x1, blocking collectives, shards(): portion = lax.all_gather(stepped, 'lon', axis=3, tiled=True)  70.2 us
    all_gather x1, blocking collectives, shards(): lax.all_gather(spectrum.astype(jnp.bfloat16), 'lat', axis=0, tiled=True)  39.7 us
    all_gather x1, blocking collectives, shards(): portion = lax.all_gather(coefs, 'lon', axis=0, tiled=True)  30.4 us
    ppermute x2, starting transfers between devices, padded(): lax.ppermute(head, axis, [((i + 1) % count, i) for i in range(count)])  13.5 us
  transfers between devices with their start and end apart: 5, of which 2 were waited for; matrix products, arithmetic and copies ran while one was open for 1% of the time, Pallas kernels for 0%

commit v1 on v0

v1 whole, which is shorter than its diff:
```python
import functools

import jax
import jax.numpy as jnp
from jax import lax
from jax.experimental import pallas as pl
from jax.experimental.pallas import tpu as pltpu
from jax.sharding import PartitionSpec as P

NLON = 2560
M = 640
ROWS = 20
GRID = 80
SLOTS = 40
LANES = 256
K = ROWS * SLOTS
CHIPS = 16
BLOCKS = 16
PACK = 48
F32 = jnp.float32
BF16 = jnp.bfloat16
MESH = pl.DeviceIdType.MESH


def fiota(shape, dim):
    return lax.broadcasted_iota(jnp.int32, shape, dim).astype(F32)


def fdiv(x, by):
    return jnp.floor((x + 0.5) * (1.0 / by))


def fmod(x, by):
    return x - by * fdiv(x, by)


def dot(a, b):
    return lax.dot_general(a, b, (((1,), (0,)), ((), ())), preferred_element_type=F32)


def dot_nt(a, b):
    return lax.dot_general(a, b, (((1,), (1,)), ((), ())), preferred_element_type=F32)


def split(x):
    high = x.astype(BF16)
    return high, (x - high.astype(F32)).astype(BF16)


def column(row, picked):
    n = row.shape[1]
    rows = picked.shape[0]
    hit = fiota((rows, n), 1) == picked
    return jnp.sum(jnp.where(hit, jnp.broadcast_to(row, (rows, n)), 0.0), axis=1, keepdims=True)


def as_row(col):
    hit = fiota((GRID, 128), 1) == fiota((GRID, 128), 0)
    return jnp.sum(jnp.where(hit, jnp.broadcast_to(col, (GRID, 128)), 0.0), axis=0, keepdims=True)


def trig(waves, first):
    lons = first + fiota((1, LANES), 1)
    turns = waves * lons
    quarter = jnp.floor(turns * (4.0 / NLON) + 0.5)
    rest = turns - quarter * (NLON / 4.0)
    t = rest * (6.283185307179586 / NLON)
    t2 = t * t
    sine = t * (1.0 + t2 * (-1.6666667e-1 + t2 * (8.3333333e-3 + t2 * (-1.9841270e-4 + t2 * 2.7557319e-6))))
    cosine = 1.0 + t2 * (-0.5 + t2 * (4.1666667e-2 + t2 * (-1.3888889e-3 + t2 * 2.4801587e-5)))
    which = quarter.astype(jnp.int32) & 3
    swap = (which & 1) == 1
    c = jnp.where(swap, sine, cosine)
    s = jnp.where(swap, cosine, sine)
    c = jnp.where((which == 1) | (which == 2), -c, c)
    s = jnp.where(which >= 2, s, -s)
    return c, s


def step_field(level, wind, up, down, at_pole, at_equator, east, west, zonal, weight, roll):
    lane = fiota((40, LANES), 1)
    wide = jnp.where(lane == 160.0, east, jnp.where(lane == 255.0, west, level))
    eastward = roll(wide, LANES - 1, 1)
    westward = roll(wide, 1, 1)
    last = level[32:40]
    row8 = fiota((8, LANES), 0)
    swapped = jnp.where(row8 == 0.0, roll(last, 1, 0), roll(last, 3, 0))
    down = jnp.where(at_equator, swapped, down)
    up = jnp.where(at_pole, 0.0, up)
    tall = jnp.concatenate([up, level, down], axis=0)
    toward = roll(tall, 54, 0)[8:48]
    poleward = roll(tall, 2, 0)[8:48]
    change = wind[0] * zonal * (eastward - westward) + 0.25 * wind[1] * (toward - poleward)
    return (level - change) * weight


def row_codes():
    r = fiota((384, 1), 0)
    parity = fdiv(r, 192.0)
    r1 = fmod(r, 192.0)
    h = fdiv(r1, 96.0)
    c = fdiv(fmod(r1, 96.0), 48.0)
    r2 = fmod(r1, 48.0)
    group = fdiv(r2, 16.0)
    level = fdiv(fmod(r2, 16.0), 8.0)
    pair = group * 8.0 + fmod(r2, 8.0)
    slot = jnp.where(pair < 20.0, 2.0 * pair + parity, -1.0)
    return slot, c, level, h


def select_rows():
    slot, c, level, h = row_codes()
    lane = fiota((1, 2 * SLOTS), 1)
    hit = (slot == fmod(lane, 40.0)) & (c == fdiv(lane, 40.0))
    return jnp.where(hit, 1.0, 0.0).astype(BF16)


def select_rows_t():
    r = fiota((1, 384), 1)
    parity = fdiv(r, 192.0)
    r1 = fmod(r, 192.0)
    c = fdiv(fmod(r1, 96.0), 48.0)
    r2 = fmod(r1, 48.0)
    pair = fdiv(r2, 16.0) * 8.0 + fmod(r2, 8.0)
    slot = jnp.where(pair < 20.0, 2.0 * pair + parity, -1.0)
    row = fiota((2 * SLOTS, 1), 0)
    hit = (slot == fmod(row, 40.0)) & (c == fdiv(row, 40.0))
    return jnp.where(hit, 1.0, 0.0).astype(BF16)


def spread_rows():
    g = fiota((128, 1), 0)
    lane = fiota((1, K), 1)
    hit = (fdiv(fmod(g, 40.0), 2.0) == fdiv(lane, 40.0)) & (g < 80.0)
    return jnp.where(hit, 1.0, 0.0).astype(BF16)


def level_mask():
    slot, c, level, h = row_codes()
    g = fiota((1, 128), 1)
    hit = (level == fdiv(g, 40.0)) & (h == fmod(g, 2.0)) & (g < 80.0)
    return hit


def slot_lanes():
    return fmod(fiota((1, K), 1), 40.0)


def reverse_matrix():
    n = fiota((M, M), 0)
    j = fiota((M, M), 1)
    hit = (n + j == M - 2.0) | (n + j == 2.0 * M - 2.0)
    return jnp.where(hit, 1.0, 0.0).astype(BF16)


def first_wave(waves, lon):
    r = fiota((64, 1), 0)
    pair = fdiv(r, 16.0) * 8.0 + fmod(r, 8.0)
    picked = jnp.where(pair < 20.0, lon * 40.0 + 2.0 * pair, -1.0)
    return column(waves, picked)


def parity_sign(first):
    j = fiota((PACK, M), 1)
    odd = (j - first).astype(jnp.int32) & 1
    return jnp.where(odd == 1, -1.0, 1.0)


def spread_weighted(weighted, selector, spreader):
    chosen = dot(selector, weighted)
    chosen = jnp.where(level_mask(), chosen, 0.0).astype(BF16)
    wide = dot(chosen, spreader)
    slot = row_codes()[0]
    return jnp.where(slot == slot_lanes(), wide, 0.0).astype(BF16)


def pack(even, odd, sign, first, c):
    lo = c * PACK
    hi = 96 + c * PACK
    kept = fiota((PACK, M), 1) >= first
    from_odd = odd[lo:lo + PACK] - sign * odd[hi:hi + PACK]
    packed = jnp.where(kept, even[lo:lo + PACK] + sign * even[hi:hi + PACK], from_odd)
    return packed, from_odd[:, M - 1:M]


def correct(total, first, lane0, extra, damping, vertical):
    j = lane0 + fiota((8, 128), 1)
    n = jnp.where(j >= first, j, (M - 2.0) - j)
    n = jnp.where(extra, M - 1.0, n)
    square = n * (n + 1.0) / float(M * M)
    raw = (total[0:8], total[8:16])
    modal = [
        (vertical[k][0] * raw[0] + vertical[k][1] * raw[1]) / (1.0 + damping[k] * square)
        for k in range(2)
    ]
    return jnp.concatenate(
        [vertical[0][l] * modal[0] + vertical[1][l] * modal[1] for l in range(2)], axis=0
    )


def unpack(packed, extra, first):
    j = fiota((PACK, M), 1)
    kept = j >= first
    even = jnp.where(kept, packed, 0.0)
    odd = jnp.where(j == M - 1.0, extra, jnp.where(kept, 0.0, packed))
    return even, odd


def spectrum_rows(even, odd, lat):
    r = fiota((32, 1), 0)
    n = jnp.where(r < ROWS, lat * ROWS + r, -5.0)
    j = fiota((1, M), 1)
    want_even = jnp.where(n == j, 1.0, 0.0).astype(BF16)
    want_odd = jnp.where((n + j == M - 2.0) | (n + j == 2.0 * M - 2.0), 1.0, 0.0).astype(BF16)
    q = fiota((96, 1), 0)
    c = fdiv(q, 48.0)
    q1 = fmod(q, 48.0)
    level = fdiv(fmod(q1, 16.0), 8.0)
    pair = fdiv(q1, 16.0) * 8.0 + fmod(q1, 8.0)
    lane = fiota((1, 160), 1)
    same = (c == fdiv(lane, 80.0)) & (level == fdiv(fmod(lane, 80.0), 40.0)) & (pair < 20.0)
    slot = fmod(lane, 40.0)
    to_even = jnp.where(same & (slot == 2.0 * pair), 1.0, 0.0).astype(BF16)
    to_odd = jnp.where(same & (slot == 2.0 * pair + 1.0), 1.0, 0.0).astype(BF16)
    return dot(dot_nt(want_even, even).astype(BF16), to_even) + dot(
        dot_nt(want_odd, odd).astype(BF16), to_odd
    )


def collapse(x_even, x_odd, selector_t, spreader):
    both = jnp.concatenate([x_even, x_odd], axis=0)
    slot = row_codes()[0]
    both = jnp.where(slot == slot_lanes(), both, 0.0).astype(BF16)
    rows = dot_nt(both, spreader)
    rows = jnp.where(level_mask(), rows, 0.0).astype(BF16)
    return dot(selector_t, rows).astype(BF16)


def kernel(
    level_ref, wind_ref, zonal_ref, weight_ref, leg_ref, wave_ref, damp_ref, vert_ref,
    grid_ref, spec_ref,
    column_out, column_in, edge_in, own_block, near_block, cos_wide, table_hi, table_lo,
    near_hi, near_lo, reversed_ref, part_out, part_in, spread_ref, packed_ref, core_in,
    sum_out, sum_in, first_ref, gathered, coefs,
    edge_send, edge_recv, near_send, near_recv, part_send, part_recv, core_send, core_recv,
    sum_send, sum_recv, all_send, all_recv, pair_send, pair_recv, coef_send, coef_recv,
    fwd_send, fwd_recv,
):
    lat = lax.axis_index("lat")
    lon = lax.axis_index("lon")
    chip = lat // 2
    core = lat % 2
    x_lo = lon // 8
    z = lon % 8
    lat_next, lat_prev = (lat + 1) % 32, (lat + 31) % 32
    lon_next, lon_prev = (lon + 1) % 16, (lon + 15) % 16
    near = (1 - x_lo) * 8 + z
    sibling = chip * 2 + 1 - core
    flat = lat.astype(F32)
    flon = lon.astype(F32)

    def chip_at(offset):
        return (chip + offset) % CHIPS

    def z_at(offset):
        return (z + offset) % 8

    def send(src, dst, send_sem, recv_sem, device):
        copy = pltpu.make_async_remote_copy(
            src_ref=src, dst_ref=dst, send_sem=send_sem, recv_sem=recv_sem,
            device_id=device, device_id_type=MESH,
        )
        copy.start()
        return copy

    def roll(x, amount, axis):
        return pltpu.roll(x, amount, axis)

    barrier = pltpu.get_barrier_semaphore()

    def greet(device):
        pl.semaphore_signal(barrier, inc=1, device_id=device, device_id_type=MESH)

    for device in (
        (lat_next, lon), (lat_prev, lon), (lat, lon_next), (lat, lon_prev), (lat, near), (sibling, lon)
    ):
        greet(device)

    @pl.loop(1, 8)
    def _(o):
        greet((lat, x_lo * 8 + z_at(o)))

    @pl.loop(1, CHIPS)
    def _(o):
        greet((chip_at(o) * 2 + core, lon))

    flat_level = jnp.reshape(level_ref[...], (GRID, LANES))
    column_out[0] = jnp.broadcast_to(as_row(flat_level[:, 0:1]), (8, 128))
    column_out[1] = jnp.broadcast_to(as_row(flat_level[:, 159:160]), (8, 128))
    waves = wave_ref[...].astype(F32)
    tall = jnp.broadcast_to(waves, (128, M))
    for t in range(5):
        cos_wide[128 * t:128 * (t + 1), :] = tall[:, 128 * t:128 * (t + 1)].T
    first_ref[...] = jnp.broadcast_to(first_wave(waves, flon), (64, 128))

    pl.semaphore_wait(barrier, 6 + 7 + 15)

    edges = [
        send(level_ref.at[:, 32:40, :], edge_in.at[0], edge_send.at[0], edge_recv.at[0], (lat_next, lon)),
        send(level_ref.at[:, 0:8, :], edge_in.at[1], edge_send.at[1], edge_recv.at[1], (lat_prev, lon)),
        send(column_out.at[0], column_in.at[0], edge_send.at[2], edge_recv.at[2], (lat, lon_prev)),
        send(column_out.at[1], column_in.at[1], edge_send.at[3], edge_recv.at[3], (lat, lon_next)),
    ]

    def fill(source, hi, lo, at, first):
        w = cos_wide[pl.ds(pl.multiple_of(source * SLOTS, 8), SLOTS), 0:1]
        c, s = trig(w, first)
        high, low = split(jnp.concatenate([c, s], axis=0))
        hi[at] = high
        lo[at] = low

    @pl.loop(0, 16)
    def _(source):
        fill(source, table_hi, table_lo, source, flon * 160.0)

    for copy in edges:
        copy.wait()

    picked = fdiv(fiota((40, 1), 0), 2.0)
    zonal = column(zonal_ref[...], picked)
    weight = column(weight_ref[...], picked) * (1.0 / float(NLON) ** 0.5)
    g = fiota((40, 1), 0)
    own_block[80:128, :] = jnp.zeros((48, LANES), F32)
    for l in range(2):
        east = column(column_in[0, 0:1, :], g + 40.0 * l)
        west = column(column_in[1, 0:1, :], g + 40.0 * l)
        own_block[40 * l:40 * (l + 1), :] = step_field(
            level_ref[l], (wind_ref[0], wind_ref[1]), edge_in[0, l], edge_in[1, l],
            lat == 0, lat == 31, east, west, zonal, weight, roll,
        )
    to_near = send(own_block, near_block, near_send, near_recv, (lat, near))

    near_first = near.astype(F32) * 160.0

    @pl.loop(0, 8)
    def _(zz):
        fill(x_lo * 8 + zz, near_hi, near_lo, zz, near_first)

    def wide(ref):
        return jnp.reshape(ref[...], (8 * 80, LANES))

    own_hi, own_lo = split(own_block[...])
    mine = pl.ds(x_lo * 8, 8)
    t_hi = jnp.reshape(table_hi[mine], (640, LANES))
    t_lo = jnp.reshape(table_lo[mine], (640, LANES))
    partial = dot_nt(t_hi, own_hi) + dot_nt(t_hi, own_lo) + dot_nt(t_lo, own_hi)
    to_near.wait()
    near_h, near_l = split(near_block[...])
    n_hi, n_lo = wide(near_hi), wide(near_lo)
    partial = partial + dot_nt(n_hi, near_h) + dot_nt(n_hi, near_l) + dot_nt(n_lo, near_h)
    part_out[...] = jnp.reshape(partial, (8, 80, 128))

    def part_copy(o):
        other = z_at(o)
        return pltpu.make_async_remote_copy(
            src_ref=part_out.at[other], dst_ref=part_in.at[z], send_sem=part_send.at[o],
            recv_sem=part_recv.at[z], device_id=(lat, x_lo * 8 + other), device_id_type=MESH,
        )

    @pl.loop(1, 8)
    def _(o):
        part_copy(o).start()

    part_in[z] = part_out[z]
    leg = leg_ref[...]
    reversed_ref[...] = dot(leg, reverse_matrix()).astype(BF16)
    sign = parity_sign(first_ref[0:PACK, 0:1])
    first = first_ref[0:PACK, 0:1]
    selector, spreader = select_rows(), spread_rows()

    @pl.loop(1, 8)
    def _(o):
        other = z_at(o)
        pltpu.make_async_remote_copy(
            src_ref=part_out.at[other], dst_ref=part_in.at[other], send_sem=part_send.at[o],
            recv_sem=part_recv.at[other], device_id=(lat, x_lo * 8 + other), device_id_type=MESH,
        ).wait_recv()

    weighted = jnp.sum(part_in[...], axis=0).astype(BF16)
    spread_ref[...] = spread_weighted(weighted, selector, spreader)
    even = dot(spread_ref[0:192], leg)
    odd = dot(spread_ref[192:384], reversed_ref[...])
    lane128 = fiota((16, 128), 1)
    for c in range(2):
        packed, extra = pack(even, odd, sign, first, c)
        rest = jnp.zeros((16, 128), F32)
        for kb in range(3):
            for t in range(5):
                packed_ref[c, kb * 5 + t] = packed[16 * kb:16 * (kb + 1), 128 * t:128 * (t + 1)]
            rest = jnp.where(lane128 == float(kb), extra[16 * kb:16 * (kb + 1)], rest)
        packed_ref[c, 15] = rest

    to_core = send(packed_ref.at[1 - core], core_in, core_send, core_recv, (sibling, lon))
    to_core.wait()
    sum_out[...] = packed_ref[core] + core_in[...]

    @pl.loop(1, CHIPS)
    def _(o):
        other = chip_at(o)
        pltpu.make_async_remote_copy(
            src_ref=sum_out.at[other], dst_ref=sum_in.at[chip], send_sem=sum_send.at[o],
            recv_sem=sum_recv.at[chip], device_id=(other * 2 + core, lon), device_id_type=MESH,
        ).start()

    sum_in[chip] = sum_out[chip]

    @pl.loop(1, CHIPS)
    def _(o):
        other = chip_at(o)
        pltpu.make_async_remote_copy(
            src_ref=sum_out.at[other], dst_ref=sum_in.at[other], send_sem=sum_send.at[o],
            recv_sem=sum_recv.at[other], device_id=(other * 2 + core, lon), device_id_type=MESH,
        ).wait_recv()

    total = jnp.sum(sum_in[...], axis=0)
    damping = (damp_ref[0], damp_ref[1])
    vertical = ((vert_ref[0, 0], vert_ref[0, 1]), (vert_ref[1, 0], vert_ref[1, 1]))
    first8 = first_ref[pl.ds(pl.multiple_of((chip // 5) * 16, 8), 8), 0:1]
    lane0 = ((chip % 5) * 128).astype(F32)
    spec = correct(total, first8, lane0, chip == 15, damping, vertical)
    gathered[core, chip] = spec.astype(BF16)

    @pl.loop(1, CHIPS)
    def _(o):
        other = chip_at(o)
        pltpu.make_async_remote_copy(
            src_ref=gathered.at[core, chip], dst_ref=gathered.at[core, chip], send_sem=all_send.at[o],
            recv_sem=all_recv.at[chip], device_id=(other * 2 + core, lon), device_id_type=MESH,
        ).start()

    @pl.loop(1, CHIPS)
    def _(o):
        other = chip_at(o)
        pltpu.make_async_remote_copy(
            src_ref=gathered.at[core, other], dst_ref=gathered.at[core, other], send_sem=all_send.at[o],
            recv_sem=all_recv.at[other], device_id=(other * 2 + core, lon), device_id_type=MESH,
        ).wait_recv()

    to_pair = send(gathered.at[core], gathered.at[core], pair_send, pair_recv, (sibling, lon))
    to_pair.wait()

    evens, odds = [], []
    for c in range(2):
        tiles = [[gathered[c, kb * 5 + t].astype(F32) for t in range(5)] for kb in range(3)]
        packed = jnp.concatenate([jnp.concatenate(row, axis=1) for row in tiles], axis=0)
        last = gathered[c, 15].astype(F32)
        extra = jnp.concatenate([last[:, kb:kb + 1] for kb in range(3)], axis=0)
        e, o = unpack(packed, extra, first)
        evens.append(e)
        odds.append(o)
    scale_even = jnp.where(first == 0.0, 1.0, 2.0)
    scale_odd = jnp.where(first == M - 1.0, 1.0, 2.0)
    north_e = [e * scale_even for e in evens]
    north_o = [o * scale_odd for o in odds]
    rows_e = jnp.concatenate(north_e + [e * sign for e in north_e], axis=0).astype(BF16)
    rows_o = jnp.concatenate(north_o + [-(o * sign) for o in north_o], axis=0).astype(BF16)
    x_even = dot_nt(rows_e, leg)
    x_odd = dot_nt(rows_o, reversed_ref[...])
    coefs[lon] = collapse(x_even, x_odd, select_rows_t(), spreader)

    def coef_copy(o):
        return pltpu.make_async_remote_copy(
            src_ref=coefs.at[lon], dst_ref=coefs.at[lon], send_sem=coef_send.at[o],
            recv_sem=coef_recv.at[z], device_id=(lat, x_lo * 8 + z_at(o)), device_id_type=MESH,
        )

    def forward_copy(source):
        at = x_lo * 8 + source
        return pltpu.make_async_remote_copy(
            src_ref=coefs.at[at], dst_ref=coefs.at[at], send_sem=fwd_send.at[source],
            recv_sem=fwd_recv.at[source], device_id=(lat, near), device_id_type=MESH,
        )

    forward_copy(z).start()

    @pl.loop(1, 8)
    def _(o):
        coef_copy(o).start()

    evens = jnp.concatenate(evens, axis=0).astype(BF16)
    odds = jnp.concatenate(odds, axis=0).astype(BF16)
    spec_ref[...] = spectrum_rows(evens, odds, flat)

    @pl.loop(1, 8)
    def _(o):
        other = z_at(o)
        at = x_lo * 8 + other
        pltpu.make_async_remote_copy(
            src_ref=coefs.at[at], dst_ref=coefs.at[at], send_sem=coef_send.at[o],
            recv_sem=coef_recv.at[other], device_id=(lat, at), device_id_type=MESH,
        ).wait_recv()
        forward_copy(other).start()

    def inverse(half):
        rows = pl.ds(half * 8, 8)
        values = jnp.reshape(coefs[rows], (640, 128)).T
        return dot(values, jnp.reshape(table_hi[rows], (640, LANES))) + dot(
            values, jnp.reshape(table_lo[rows], (640, LANES))
        )

    grid = inverse(x_lo)

    @pl.loop(0, 8)
    def _(source):
        at = (1 - x_lo) * 8 + source
        pltpu.make_async_remote_copy(
            src_ref=coefs.at[at], dst_ref=coefs.at[at], send_sem=fwd_send.at[source],
            recv_sem=fwd_recv.at[source], device_id=(lat, near), device_id_type=MESH,
        ).wait_recv()

    grid = grid + inverse(1 - x_lo)
    grid_ref[...] = grid[0:GRID] * (1.0 / float(NLON * M) ** 0.5)

    @pl.loop(1, 8)
    def _(o):
        part_copy(o).wait_send()
        coef_copy(o).wait_send()

    @pl.loop(0, 8)
    def _(source):
        forward_copy(source).wait_send()

    @pl.loop(1, CHIPS)
    def _(o):
        other = chip_at(o)
        pltpu.make_async_remote_copy(
            src_ref=sum_out.at[other], dst_ref=sum_in.at[chip], send_sem=sum_send.at[o],
            recv_sem=sum_recv.at[chip], device_id=(other * 2 + core, lon), device_id_type=MESH,
        ).wait_send()
        pltpu.make_async_remote_copy(
            src_ref=gathered.at[core, chip], dst_ref=gathered.at[core, chip], send_sem=all_send.at[o],
            recv_sem=all_recv.at[chip], device_id=(other * 2 + core, lon), device_id_type=MESH,
        ).wait_send()


def shards(level_fields, wind_field, zonal_step, quad_weight, legendre, wave_table, damping, vertical):
    def rows(x):
        x = x.transpose(0, 2, 1, 3).reshape(2, 2 * ROWS, 160)
        return jnp.pad(x, ((0, 0), (0, 0), (0, LANES - 160)))

    vmem = pl.BlockSpec(memory_space=pltpu.VMEM)
    smem = pl.BlockSpec(memory_space=pltpu.SMEM)
    dma = pltpu.SemaphoreType.DMA
    grid, spec = pl.pallas_call(
        kernel,
        out_shape=(
            jax.ShapeDtypeStruct((GRID, LANES), F32),
            jax.ShapeDtypeStruct((32, 160), F32),
        ),
        in_specs=[vmem] * 6 + [smem] * 2,
        out_specs=(vmem, vmem),
        scratch_shapes=[
            pltpu.VMEM((2, 8, 128), F32),
            pltpu.VMEM((2, 8, 128), F32),
            pltpu.VMEM((2, 2, 8, LANES), F32),
            pltpu.VMEM((128, LANES), F32),
            pltpu.VMEM((128, LANES), F32),
            pltpu.VMEM((M, 128), F32),
            pltpu.VMEM((16, 80, LANES), BF16),
            pltpu.VMEM((16, 80, LANES), BF16),
            pltpu.VMEM((8, 80, LANES), BF16),
            pltpu.VMEM((8, 80, LANES), BF16),
            pltpu.VMEM((K, M), BF16),
            pltpu.VMEM((8, 80, 128), F32),
            pltpu.VMEM((8, 80, 128), F32),
            pltpu.VMEM((384, K), BF16),
            pltpu.VMEM((2, BLOCKS, 16, 128), F32),
            pltpu.VMEM((BLOCKS, 16, 128), F32),
            pltpu.VMEM((BLOCKS, 16, 128), F32),
            pltpu.VMEM((CHIPS, 16, 128), F32),
            pltpu.VMEM((64, 128), F32),
            pltpu.VMEM((2, BLOCKS, 16, 128), BF16),
            pltpu.VMEM((16, 80, 128), BF16),
            dma((4,)), dma((4,)), dma, dma, dma((8,)), dma((8,)), dma, dma,
            dma((CHIPS,)), dma((CHIPS,)), dma((CHIPS,)), dma((CHIPS,)), dma, dma,
            dma((8,)), dma((8,)), dma((8,)), dma((8,)),
        ],
        compiler_params=pltpu.CompilerParams(
            collective_id=0, has_side_effects=True, vmem_limit_bytes=40 * 1024 * 1024
        ),
    )(
        rows(level_fields), rows(wind_field), zonal_step[None], quad_weight[None],
        legendre.transpose(1, 0, 2).reshape(K, M), wave_table[None], damping, vertical,
    )
    fields = grid[:, :160].reshape(2, ROWS, 2, 160).transpose(0, 2, 1, 3)
    spectrum = spec[:ROWS].reshape(ROWS, 2, 2, SLOTS).transpose(0, 3, 1, 2)
    return fields, spectrum


def solution(mesh):
    return jax.shard_map(
        shards,
        mesh=mesh,
        in_specs=(
            P(None, None, "lat", "lon"),
            P(None, None, "lat", "lon"),
            P("lat"),
            P("lat"),
            P("lon", "lat", None),
            P(),
            P(),
            P(),
        ),
        out_specs=(P(None, None, "lat", "lon"), P("lat", "lon", None, None)),
        check_vma=False,
    )
```

time: 505 us -> 70.6 us (0.14); the launches traced: 499 us -> 70.3 us
  waiting for transfers between devices: 280 us -> 0 us
  blocking collectives: 140 us -> 0 us
  Pallas kernels: 0 us -> 63.7 us
  starting transfers between devices: 20.1 us -> 0 us
  local copies, waits for them, and re-layouts: 20.7 us -> 5.84 us
  matrix products: 14.6 us -> 0 us
  between operations: 15.1 us -> 0.71 us
  other arithmetic: 8.39 us -> 0 us
    unnamed x2 -> x0, waiting for transfers between devices: 276 us -> none
    all_gather x3 -> x0, blocking collectives: 140 us -> none  [the longest x1 70.2 us: shards(): portion = lax.all_gather(stepped, 'lon', axis=3, tiled=True)]
    pallas_call x0 -> x1, Pallas kernels: none -> 63.7 us  [shards(): pl.pallas_call(kernel, out_shape=(jax.ShapeDtypeStruct((GRID, LANES), F32...]
    ppermute x4 -> x0, starting transfers between devices: 20 us -> none  [the longest x2 13.5 us: padded(): lax.ppermute(head, axis, [((i + 1) % count, i) for i in range(count)])]
    dot_general x9 -> x0, matrix products: 14.6 us -> none  [the longest x1 3.2 us: shards(): lax.dot_general(portion[:, 1], jnp.sin(angles) * factor, contract_first,...]
    unnamed x24 -> x14, local copies, waits for them, and re-layouts: 9.49 us -> 3.42 us
    all_gather x1 -> x0, local copies, waits for them, and re-layouts: 5.68 us -> none  [shards(): portion = lax.all_gather(stepped, 'lon', axis=3, tiled=True)]
  transfers between devices with their start and end apart: 5 -> 0, of which waited for: 2 -> 0; matrix products, arithmetic and copies ran while one was open for 1% -> 0% of each run, Pallas kernels for 0% -> 0%
where the time goes in v1:
time: 70.6 us; the launch traced here: 70.3 us
  Pallas kernels  63.7 us (90%)
  local copies, waits for them, and re-layouts  5.84 us (8%)
  between operations  0.71 us (1%)
    pallas_call x1, Pallas kernels, shards(): pl.pallas_call(kernel, out_shape=(jax.ShapeDtypeStruct((GRID, LANES), F32...  63.7 us
    unnamed x14, local copies, waits for them, and re-layouts  3.42 us

profile of v1, /device:TPU:1, one launch (start us, length us, event | category | flops | bytes accessed | tf_op | source)
XLA Modules:
  0.0 70.3 jit_solution(7583351634970459653)
XLA Ops:
  0.6 0.0 copy-start.6
  0.6 0.7 copy-done.6
  1.3 0.9 %reshape.19 = f32[2,40,160]{2,1,0:T(8,128)S(1)} reshape(f32[2,20,2,160]{3,2,1,0:T(2,128)} %bitcast.14) | data formatting | bytes 102400 | tf_op jit(solution)/shard_map/reshape | solution.py:548
  2.3 0.0 copy-start.5
  2.3 0.9 %copy-done.5 = f32[2,2,20,160]{3,1,2,0:T(2,128)S(1)} copy-done((f32[2,2,20,160]{3,1,2,0:T(2,128)S(1)}, f32[2,2,20,160]{3,1,2,0:T(2,128)}, u32[]{:S(2)}) %copy-start.5) | copy-done | bytes 51224
  3.2 0.1 reshape.20
  3.2 0.0 copy-start.1
  3.2 0.0 copy-start.2
  3.2 0.0 copy-start.3
  3.3 0.0 copy-start.4
  3.3 0.6 copy-done.1
  3.9 0.0 copy-done.2
  3.9 0.0 copy-done.3
  3.9 0.0 copy-done.4
  3.9 0.0 copy-start
  3.9 1.2 %copy-done = bf16[40,20,640]{2,0,1:T(8,128)(2,1)S(1)} copy-done((bf16[40,20,640]{2,0,1:T(8,128)(2,1)S(1)}, bf16[40,20,640]{2,0,1:T(8,128)(2,1)}, u32[]{:S(2)}) %copy-start) | copy-done | bytes 1024024
  5.1 63.7 %shard_map.95 = (f32[80,256]{1,0:T(8,128)S(1)}, f32[32,160]{1,0:T(8,128)S(1)}) custom-call(f32[2,40,256]{2,1,0:T(8,128)S(1)} %pad.7.level_ref, f32[2,40,256]{2,1,0:T(8,128)S(1)} %pad.8.wind_ref, f32[1,20]{1,0:T(1,128)S(1)} %bitcast.12, f32[1,20]{1,0:T(1,128)S(1)} %bitcast.13, bf16[800,640]{1,0:T(8,128)(2,1)S(1)} %bitcast.10, ...), custom_call_target="tpu_custom_call" | custom-call | tf_op jit(solution)/shard_map/pallas_call | solution.py:554
  68.9 0.7 reshape.22
  69.6 0.7 %reshape.23 = f32[20,2,2,40]{3,2,1,0:T(2,128)} reshape(f32[20,160]{1,0:T(8,128)S(1)} %slice.7) | data formatting | bytes 25600 | tf_op jit(solution)/shard_map/reshape | solution.py:596
  (4 shorter events, 0.0 us)
Async XLA Ops:
  0.6 0.7 copy-start.6
  2.3 0.9 %copy-start.5 = (f32[2,2,20,160]{3,1,2,0:T(2,128)S(1)}, f32[2,2,20,160]{3,1,2,0:T(2,128)}, u32[]{:S(2)}) copy-start(f32[2,2,20,160]{3,1,2,0:T(2,128)} %param.9) | copy-start | bytes 153604
  3.2 0.7 copy-start.1
  3.2 0.7 copy-start.2
  3.2 0.7 copy-start.3
  3.3 0.7 copy-start.4
  3.9 1.2 %copy-start = (bf16[40,20,640]{2,0,1:T(8,128)(2,1)S(1)}, bf16[40,20,640]{2,0,1:T(8,128)(2,1)}, u32[]{:S(2)}) copy-start(bf16[40,20,640]{2,0,1:T(8,128)(2,1)} %param.12) | copy-start | bytes 3072004

commit v2 on v1

--- a/solution.py
+++ b/solution.py
@@ -20,6 +20,8 @@
 F32 = jnp.float32
 BF16 = jnp.bfloat16
 MESH = pl.DeviceIdType.MESH
+FAR_FIRST = (12, 11, 13, 4, 10, 14, 3, 5, 9, 15, 8, 2, 6, 1, 7)
+Z_FAR_FIRST = (4, 3, 5, 2, 6, 1, 7)
 
 
 def fiota(shape, dim):
@@ -237,14 +239,15 @@
 
 
 def kernel(
-    level_ref, wind_ref, zonal_ref, weight_ref, leg_ref, wave_ref, damp_ref, vert_ref,
+    level_hbm, wind_hbm, zonal_hbm, weight_hbm, leg_hbm, wave_hbm, damp_hbm, vert_hbm,
     grid_ref, spec_ref,
-    column_out, column_in, edge_in, own_block, near_block, cos_wide, table_hi, table_lo,
-    near_hi, near_lo, reversed_ref, part_out, part_in, spread_ref, packed_ref, core_in,
-    sum_out, sum_in, first_ref, gathered, coefs,
-    edge_send, edge_recv, near_send, near_recv, part_send, part_recv, core_send, core_recv,
-    sum_send, sum_recv, all_send, all_recv, pair_send, pair_recv, coef_send, coef_recv,
-    fwd_send, fwd_recv,
+    native, zonal_ref, weight_ref, leg_ref, wave_ref, damp_ref, vert_ref,
+    field_ref, field_near, column_out, column_in, edge_in, own_block, near_block, wave_col,
+    table_hi, table_lo, near_hi, near_lo, reversed_ref, part_out, part_in, spread_ref,
+    packed_ref, core_in, sum_out, sum_in, first_ref, gathered, coefs,
+    load_sem, edge_send, edge_recv, near_send, near_recv, part_send, part_recv, core_send,
+    core_recv, sum_send, sum_recv, all_send, all_recv, pair_send, pair_recv, coef_send,
+    coef_recv, fwd_send, fwd_recv, heard,
 ):
     lat = lax.axis_index("lat")
     lon = lax.axis_index("lon")
@@ -254,13 +257,19 @@
     z = lon % 8
     lat_next, lat_prev = (lat + 1) % 32, (lat + 31) % 32
     lon_next, lon_prev = (lon + 1) % 16, (lon + 15) % 16
-    near = (1 - x_lo) * 8 + z
+    near = (lon + 8) % 16
     sibling = chip * 2 + 1 - core
     flat = lat.astype(F32)
     flon = lon.astype(F32)
 
     def chip_at(offset):
-        return (chip + offset) % CHIPS
+        return (chip // 8 * 8 + offset // 8 * 8) % CHIPS + (chip + offset) % 8
+
+    def y_at(offset):
+        return ((chip // 8) * 8 + (chip + offset) % 8) * 2 + core
+
+    def tell(sem, device):
+        pl.semaphore_signal(sem, inc=1, device_id=device, device_id_type=MESH)
 
     def z_at(offset):
         return (z + offset) % 8
@@ -281,82 +290,123 @@
     def greet(device):
         pl.semaphore_signal(barrier, inc=1, device_id=device, device_id_type=MESH)
 
-    for device in (
-        (lat_next, lon), (lat_prev, lon), (lat, lon_next), (lat, lon_prev), (lat, near), (sibling, lon)
-    ):
-        greet(device)
+    loads = [
+        pltpu.make_async_copy(src, dst, load_sem.at[n])
+        for n, (src, dst) in enumerate((
+            (level_hbm, native.at[0]), (wind_hbm, native.at[1]), (wave_hbm, wave_ref),
+            (zonal_hbm, zonal_ref), (weight_hbm, weight_ref), (damp_hbm, damp_ref),
+            (vert_hbm, vert_ref), (leg_hbm, leg_ref),
+        ))
+    ]
+    for copy in loads:
+        copy.start()
+
+    across = ((chip + 8) % CHIPS * 2 + core, lon)
+    greet(across)
+    for step in (1, 7):
+        greet((y_at(step), lon))
 
     @pl.loop(1, 8)
     def _(o):
         greet((lat, x_lo * 8 + z_at(o)))
 
-    @pl.loop(1, CHIPS)
-    def _(o):
-        greet((chip_at(o) * 2 + core, lon))
-
-    flat_level = jnp.reshape(level_ref[...], (GRID, LANES))
+    edge_devices = (
+        ((lat_next, lon), 0, 0), ((lat_prev, lon), 0, 1), ((lat_next, near), 1, 0), ((lat_prev, near), 1, 1),
+        ((lat, lon_prev), 0, 0), ((lat, lon_next), 0, 1),
+        ((lat, (lon_prev + 8) % 16), 1, 0), ((lat, (lon_next + 8) % 16), 1, 1),
+    )
+    for device, _, _ in edge_devices:
+        greet(device)
+    greet((lat, near))
+
+    for copy in loads[:7]:
+        copy.wait()
+
+    field_ref[:, :, 128:LANES] = jnp.zeros((4, 40, 128), F32)
+    for a in range(2):
+        for b in range(2):
+            for i in range(ROWS):
+                field_ref[2 * a + b, 2 * i:2 * i + 2, 0:160] = native[a, b, i]
+
+    flat_level = jnp.reshape(field_ref[0:2], (GRID, LANES))
     column_out[0] = jnp.broadcast_to(as_row(flat_level[:, 0:1]), (8, 128))
     column_out[1] = jnp.broadcast_to(as_row(flat_level[:, 159:160]), (8, 128))
     waves = wave_ref[...].astype(F32)
-    tall = jnp.broadcast_to(waves, (128, M))
+    waves = [waves[t:t + 1, :] for t in range(5)]
     for t in range(5):
-        cos_wide[128 * t:128 * (t + 1), :] = tall[:, 128 * t:128 * (t + 1)].T
+        wave_col[128 * t:128 * (t + 1), :] = jnp.broadcast_to(waves[t], (128, 128)).T
+    waves = jnp.concatenate(waves, axis=1)
     first_ref[...] = jnp.broadcast_to(first_wave(waves, flon), (64, 128))
 
-    pl.semaphore_wait(barrier, 6 + 7 + 15)
-
-    edges = [
-        send(level_ref.at[:, 32:40, :], edge_in.at[0], edge_send.at[0], edge_recv.at[0], (lat_next, lon)),
-        send(level_ref.at[:, 0:8, :], edge_in.at[1], edge_send.at[1], edge_recv.at[1], (lat_prev, lon)),
-        send(column_out.at[0], column_in.at[0], edge_send.at[2], edge_recv.at[2], (lat, lon_prev)),
-        send(column_out.at[1], column_in.at[1], edge_send.at[3], edge_recv.at[3], (lat, lon_next)),
-    ]
-
     def fill(source, hi, lo, at, first):
-        w = cos_wide[pl.ds(pl.multiple_of(source * SLOTS, 8), SLOTS), 0:1]
+        w = wave_col[pl.ds(pl.multiple_of(source * SLOTS, 8), SLOTS), 0:1]
         c, s = trig(w, first)
         high, low = split(jnp.concatenate([c, s], axis=0))
         hi[at] = high
         lo[at] = low
 
-    @pl.loop(0, 16)
-    def _(source):
-        fill(source, table_hi, table_lo, source, flon * 160.0)
-
-    for copy in edges:
-        copy.wait()
+    near_first = near.astype(F32) * 160.0
+
+    @pl.loop(0, 8)
+    def _(zz):
+        fill(x_lo * 8 + zz, table_hi, table_lo, x_lo * 8 + zz, flon * 160.0)
+        fill(x_lo * 8 + zz, near_hi, near_lo, zz, near_first)
+
+    pl.semaphore_wait(barrier, 3 + 7 + 9)
+
+    to_near = send(field_ref, field_near, near_send, near_recv, (lat, near))
+    edges = []
+    for n, (device, block, side) in enumerate(edge_devices):
+        if n < 4:
+            src = field_ref.at[0:2, 32:40, :] if side == 0 else field_ref.at[0:2, 0:8, :]
+            dst = edge_in.at[block, side]
+        else:
+            src, dst = column_out.at[side], column_in.at[block, side]
+        edges.append(send(src, dst, edge_send.at[n], edge_recv.at[n], device))
+
+    for step in (1, 7):
+        tell(heard.at[0], (y_at(step), lon))
 
     picked = fdiv(fiota((40, 1), 0), 2.0)
     zonal = column(zonal_ref[...], picked)
     weight = column(weight_ref[...], picked) * (1.0 / float(NLON) ** 0.5)
     g = fiota((40, 1), 0)
     own_block[80:128, :] = jnp.zeros((48, LANES), F32)
-    for l in range(2):
-        east = column(column_in[0, 0:1, :], g + 40.0 * l)
-        west = column(column_in[1, 0:1, :], g + 40.0 * l)
-        own_block[40 * l:40 * (l + 1), :] = step_field(
-            level_ref[l], (wind_ref[0], wind_ref[1]), edge_in[0, l], edge_in[1, l],
-            lat == 0, lat == 31, east, west, zonal, weight, roll,
-        )
-    to_near = send(own_block, near_block, near_send, near_recv, (lat, near))
-
-    near_first = near.astype(F32) * 160.0
-
-    @pl.loop(0, 8)
-    def _(zz):
-        fill(x_lo * 8 + zz, near_hi, near_lo, zz, near_first)
+    near_block[80:128, :] = jnp.zeros((48, LANES), F32)
+    first = first_ref[0:PACK, 0:1]
+    sign = parity_sign(first)
+    selector, spreader = select_rows(), spread_rows()
+
+    for copy in edges:
+        copy.wait()
+    to_near.wait()
+
+    pl.semaphore_wait(heard.at[0], 2)
+    for step in (2, 6):
+        tell(heard.at[1], (y_at(step), lon))
+
+    def advance(block, field, out):
+        for l in range(2):
+            east = column(column_in[block, 0, 0:1, :], g + 40.0 * l)
+            west = column(column_in[block, 1, 0:1, :], g + 40.0 * l)
+            out[40 * l:40 * (l + 1), :] = step_field(
+                field[l], (field[2], field[3]), edge_in[block, 0, l], edge_in[block, 1, l],
+                lat == 0, lat == 31, east, west, zonal, weight, roll,
+            )
+
+    advance(0, field_ref, own_block)
+    advance(1, field_near, near_block)
 
     def wide(ref):
         return jnp.reshape(ref[...], (8 * 80, LANES))
 
     own_hi, own_lo = split(own_block[...])
+    near_h, near_l = split(near_block[...])
     mine = pl.ds(x_lo * 8, 8)
     t_hi = jnp.reshape(table_hi[mine], (640, LANES))
     t_lo = jnp.reshape(table_lo[mine], (640, LANES))
+    n_hi, n_lo = wide(near_hi), wide(near_lo)
     partial = dot_nt(t_hi, own_hi) + dot_nt(t_hi, own_lo) + dot_nt(t_lo, own_hi)
-    to_near.wait()
-    near_h, near_l = split(near_block[...])
-    n_hi, n_lo = wide(near_hi), wide(near_lo)
     partial = partial + dot_nt(n_hi, near_h) + dot_nt(n_hi, near_l) + dot_nt(n_lo, near_h)
     part_out[...] = jnp.reshape(partial, (8, 80, 128))
 
@@ -367,16 +417,15 @@
             recv_sem=part_recv.at[z], device_id=(lat, x_lo * 8 + other), device_id_type=MESH,
         )
 
-    @pl.loop(1, 8)
-    def _(o):
+    for o in Z_FAR_FIRST:
         part_copy(o).start()
 
+    pl.semaphore_wait(heard.at[1], 2)
+    tell(heard.at[2], across)
     part_in[z] = part_out[z]
+    loads[7].wait()
     leg = leg_ref[...]
     reversed_ref[...] = dot(leg, reverse_matrix()).astype(BF16)
-    sign = parity_sign(first_ref[0:PACK, 0:1])
-    first = first_ref[0:PACK, 0:1]
-    selector, spreader = select_rows(), spread_rows()
 
     @pl.loop(1, 8)
     def _(o):
@@ -403,16 +452,25 @@
     to_core = send(packed_ref.at[1 - core], core_in, core_send, core_recv, (sibling, lon))
     to_core.wait()
     sum_out[...] = packed_ref[core] + core_in[...]
-
-    @pl.loop(1, CHIPS)
-    def _(o):
+    pl.semaphore_wait(heard.at[2], 1)
+
+    def sum_copy(o):
         other = chip_at(o)
-        pltpu.make_async_remote_copy(
+        return pltpu.make_async_remote_copy(
             src_ref=sum_out.at[other], dst_ref=sum_in.at[chip], send_sem=sum_send.at[o],
             recv_sem=sum_recv.at[chip], device_id=(other * 2 + core, lon), device_id_type=MESH,
-        ).start()
+        )
+
+    for o in FAR_FIRST:
+        sum_copy(o).start()
 
     sum_in[chip] = sum_out[chip]
+
+    @pl.loop(0, 8)
+    def _(zz):
+        source = (1 - x_lo) * 8 + zz
+        fill(source, table_hi, table_lo, source, flon * 160.0)
+
 
     @pl.loop(1, CHIPS)
     def _(o):
@@ -430,13 +488,14 @@
     spec = correct(total, first8, lane0, chip == 15, damping, vertical)
     gathered[core, chip] = spec.astype(BF16)
 
-    @pl.loop(1, CHIPS)
-    def _(o):
-        other = chip_at(o)
-        pltpu.make_async_remote_copy(
+    def all_copy(o):
+        return pltpu.make_async_remote_copy(
             src_ref=gathered.at[core, chip], dst_ref=gathered.at[core, chip], send_sem=all_send.at[o],
-            recv_sem=all_recv.at[chip], device_id=(other * 2 + core, lon), device_id_type=MESH,
-        ).start()
+            recv_sem=all_recv.at[chip], device_id=(chip_at(o) * 2 + core, lon), device_id_type=MESH,
+        )
+
+    for o in FAR_FIRST:
+        all_copy(o).start()
 
     @pl.loop(1, CHIPS)
     def _(o):
@@ -483,8 +542,7 @@
 
     forward_copy(z).start()
 
-    @pl.loop(1, 8)
-    def _(o):
+    for o in Z_FAR_FIRST:
         coef_copy(o).start()
 
     evens = jnp.concatenate(evens, axis=0).astype(BF16)
@@ -532,24 +590,16 @@
 
     @pl.loop(1, CHIPS)
     def _(o):
-        other = chip_at(o)
-        pltpu.make_async_remote_copy(
-            src_ref=sum_out.at[other], dst_ref=sum_in.at[chip], send_sem=sum_send.at[o],
-            recv_sem=sum_recv.at[chip], device_id=(other * 2 + core, lon), device_id_type=MESH,
-        ).wait_send()
-        pltpu.make_async_remote_copy(
-            src_ref=gathered.at[core, chip], dst_ref=gathered.at[core, chip], send_sem=all_send.at[o],
-            recv_sem=all_recv.at[chip], device_id=(other * 2 + core, lon), device_id_type=MESH,
-        ).wait_send()
+        sum_copy(o).wait_send()
+        all_copy(o).wait_send()
 
 
 def shards(level_fields, wind_field, zonal_step, quad_weight, legendre, wave_table, damping, vertical):
     def rows(x):
-        x = x.transpose(0, 2, 1, 3).reshape(2, 2 * ROWS, 160)
-        return jnp.pad(x, ((0, 0), (0, 0), (0, LANES - 160)))
+        return x.transpose(0, 2, 1, 3)
 
     vmem = pl.BlockSpec(memory_space=pltpu.VMEM)
-    smem = pl.BlockSpec(memory_space=pltpu.SMEM)
+    hbm = pl.BlockSpec(memory_space=pl.ANY)
     dma = pltpu.SemaphoreType.DMA
     grid, spec = pl.pallas_call(
         kernel,
@@ -557,12 +607,21 @@
             jax.ShapeDtypeStruct((GRID, LANES), F32),
             jax.ShapeDtypeStruct((32, 160), F32),
         ),
-        in_specs=[vmem] * 6 + [smem] * 2,
+        in_specs=[hbm] * 8,
         out_specs=(vmem, vmem),
         scratch_shapes=[
+            pltpu.VMEM((2, 2, ROWS, 2, 160), F32),
+            pltpu.VMEM((1, ROWS), F32),
+            pltpu.VMEM((1, ROWS), F32),
+            pltpu.VMEM((K, M), BF16),
+            pltpu.VMEM((5, 128), jnp.int32),
+            pltpu.SMEM((2,), F32),
+            pltpu.SMEM((2, 2), F32),
+            pltpu.VMEM((4, 40, LANES), F32),
+            pltpu.VMEM((4, 40, LANES), F32),
             pltpu.VMEM((2, 8, 128), F32),
-            pltpu.VMEM((2, 8, 128), F32),
-            pltpu.VMEM((2, 2, 8, LANES), F32),
+            pltpu.VMEM((2, 2, 8, 128), F32),
+            pltpu.VMEM((2, 2, 2, 8, LANES), F32),
             pltpu.VMEM((128, LANES), F32),
             pltpu.VMEM((128, LANES), F32),
             pltpu.VMEM((M, 128), F32),
@@ -581,16 +640,17 @@
             pltpu.VMEM((64, 128), F32),
             pltpu.VMEM((2, BLOCKS, 16, 128), BF16),
             pltpu.VMEM((16, 80, 128), BF16),
-            dma((4,)), dma((4,)), dma, dma, dma((8,)), dma((8,)), dma, dma,
+            dma((8,)), dma((8,)), dma((8,)), dma, dma, dma((8,)), dma((8,)), dma, dma,
             dma((CHIPS,)), dma((CHIPS,)), dma((CHIPS,)), dma((CHIPS,)), dma, dma,
             dma((8,)), dma((8,)), dma((8,)), dma((8,)),
+            pltpu.SemaphoreType.REGULAR((3,)),
         ],
         compiler_params=pltpu.CompilerParams(
-            collective_id=0, has_side_effects=True, vmem_limit_bytes=40 * 1024 * 1024
+            collective_id=0, has_side_effects=True, vmem_limit_bytes=60 * 1024 * 1024
         ),
     )(
         rows(level_fields), rows(wind_field), zonal_step[None], quad_weight[None],
-        legendre.transpose(1, 0, 2).reshape(K, M), wave_table[None], damping, vertical,
+        legendre.transpose(1, 0, 2).reshape(K, M), wave_table.reshape(5, 128), damping, vertical,
     )
     fields = grid[:, :160].reshape(2, ROWS, 2, 160).transpose(0, 2, 1, 3)
     spectrum = spec[:ROWS].reshape(ROWS, 2, 2, SLOTS).transpose(0, 3, 1, 2)

time: 70.6 us -> 63.3 us (0.90)
  local copies, waits for them, and re-layouts: 5.84 us -> 2.3 us
  Pallas kernels: 63.7 us -> 60.2 us
    pallas_call x1, Pallas kernels: 63.7 us -> 60.2 us  [shards(): pl.pallas_call(kernel, out_shape=(jax.ShapeDtypeStruct((GRID, LANES), F32...]
    unnamed x14 -> x2, local copies, waits for them, and re-layouts: 3.42 us -> 0.01 us
    reshape x2 -> x0, local copies, waits for them, and re-layouts: 1 us -> none  [rows(): x = x.transpose(0, 2, 1, 3).reshape(2, 2 * ROWS, 160)]
    reshape x1, local copies, waits for them, and re-layouts: 0.68 us -> 1.57 us  [shards(): fields = grid[:, :160].reshape(2, ROWS, 2, 160).transpose(0, 2, 1, 3)]
where the time goes in v2:
time: 63.3 us; the launch traced here: 63.2 us
  Pallas kernels  60.2 us (95%)
  local copies, waits for them, and re-layouts  2.3 us (4%)
  between operations  0.65 us (1%)
    pallas_call x1, Pallas kernels, shards(): pl.pallas_call(kernel, out_shape=(jax.ShapeDtypeStruct((GRID, LANES), F32...  60.2 us
    reshape x1, local copies, waits for them, and re-layouts, shards(): fields = grid[:, :160].reshape(2, ROWS, 2, 160).transpose(0, 2, 1, 3)  1.57 us

profile of v2, /device:TPU:1, one launch (start us, length us, event | category | flops | bytes accessed | tf_op | source)
XLA Modules:
  0.0 63.2 jit_solution(8845581630885097490)
XLA Ops:
  0.6 60.2 %shard_map.95 = (f32[80,256]{1,0:T(8,128)}, f32[32,160]{1,0:T(8,128)}) custom-call(f32[2,20,2,160]{3,2,1,0:T(2,128)} %bitcast.12, f32[2,20,2,160]{3,2,1,0:T(2,128)} %bitcast.13, f32[1,20]{1,0:T(1,128)} %bitcast.18, f32[1,20]{1,0:T(1,128)} %bitcast.19, bf16[800,640]{1,0:T(8,128)(2,1)} %bitcast.11, s32[5,128]{1,0:T(8,128)} %bitcast.17, f32[2]{0:T(128)} %damp_hbm.1, ...), custom_call_target="tpu_custom_call" | custom-call | tf_op jit(solution)/shard_map/pallas_call | solution.py:604
  60.9 0.0 copy-start
  60.9 1.6 %reshape.18 = f32[2,20,2,160]{3,2,1,0:T(2,128)} reshape(f32[80,160]{1,0:T(8,128)} %bitcast.15) | data formatting | bytes 102400 | tf_op jit(solution)/shard_map/reshape | solution.py:655
  62.4 0.0 copy-done
  62.4 0.7 %reshape.19 = f32[20,2,2,40]{3,2,1,0:T(2,128)} reshape(f32[20,160]{1,0:T(8,128)S(1)} %slice.7) | data formatting | bytes 25600 | tf_op jit(solution)/shard_map/reshape | solution.py:656
  (1 shorter events, 0.0 us)
Async XLA Ops:
  60.9 1.6 %copy-start = (f32[32,160]{1,0:T(8,128)S(1)}, f32[32,160]{1,0:T(8,128)}, u32[]{:S(2)}) copy-start(f32[32,160]{1,0:T(8,128)} %get-tuple-element.5) | copy-start | bytes 61444

commit v3 on v2

--- a/solution.py
+++ b/solution.py
@@ -17,6 +17,8 @@
 CHIPS = 16
 BLOCKS = 16
 PACK = 48
+FOLDED = 56
+FOLDED16 = 64
 F32 = jnp.float32
 BF16 = jnp.bfloat16
 MESH = pl.DeviceIdType.MESH
@@ -96,8 +98,7 @@
     return (level - change) * weight
 
 
-def row_codes():
-    r = fiota((384, 1), 0)
+def row_codes(r):
     parity = fdiv(r, 192.0)
     r1 = fmod(r, 192.0)
     h = fdiv(r1, 96.0)
@@ -110,38 +111,70 @@
     return slot, c, level, h
 
 
+def folded_rows(slot, c):
+    rest = 40.0 + fmod(slot, 8.0) + 8.0 * fdiv(slot, 32.0)
+    return slot, jnp.where((c == 1.0) & (slot >= 0.0), rest, -1.0)
+
+
 def select_rows():
-    slot, c, level, h = row_codes()
-    lane = fiota((1, 2 * SLOTS), 1)
-    hit = (slot == fmod(lane, 40.0)) & (c == fdiv(lane, 40.0))
+    slot, c, level, h = row_codes(fiota((384, 1), 0))
+    lane = fiota((1, FOLDED), 1)
+    return tuple(jnp.where(r == lane, 1.0, 0.0).astype(BF16) for r in folded_rows(slot, c))
+
+
+def select_rows_t():
+    slot, c, level, h = row_codes(fiota((1, 384), 1))
+    row = fiota((FOLDED16, 1), 0)
+    return tuple(jnp.where(r == row, 1.0, 0.0).astype(BF16) for r in folded_rows(slot, c))
+
+
+def spread_rows():
+    lane = fiota((256, 1), 0)
+    g = jnp.where(lane < 80.0, lane, jnp.where(lane < 128.0, lane - 80.0, 48.0 + fmod(lane, 32.0)))
+    hit = fdiv(fmod(g, 40.0), 2.0) == fdiv(fiota((1, K), 1), 40.0)
     return jnp.where(hit, 1.0, 0.0).astype(BF16)
 
 
-def select_rows_t():
-    r = fiota((1, 384), 1)
-    parity = fdiv(r, 192.0)
-    r1 = fmod(r, 192.0)
-    c = fdiv(fmod(r1, 96.0), 48.0)
-    r2 = fmod(r1, 48.0)
-    pair = fdiv(r2, 16.0) * 8.0 + fmod(r2, 8.0)
-    slot = jnp.where(pair < 20.0, 2.0 * pair + parity, -1.0)
-    row = fiota((2 * SLOTS, 1), 0)
-    hit = (slot == fmod(row, 40.0)) & (c == fdiv(row, 40.0))
-    return jnp.where(hit, 1.0, 0.0).astype(BF16)
-
-
-def spread_rows():
-    g = fiota((128, 1), 0)
-    lane = fiota((1, K), 1)
-    hit = (fdiv(fmod(g, 40.0), 2.0) == fdiv(lane, 40.0)) & (g < 80.0)
-    return jnp.where(hit, 1.0, 0.0).astype(BF16)
-
-
 def level_mask():
-    slot, c, level, h = row_codes()
-    g = fiota((1, 128), 1)
-    hit = (level == fdiv(g, 40.0)) & (h == fmod(g, 2.0)) & (g < 80.0)
-    return hit
+    slot, c, level, h = row_codes(fiota((384, 1), 0))
+    lane = fiota((1, 256), 1)
+    rest = lane >= 128.0
+    g = jnp.where(lane < 80.0, lane, jnp.where(rest, 48.0 + fmod(lane, 32.0), lane - 80.0))
+    part = jnp.where(lane < 80.0, 0.0, 1.0)
+    group = jnp.where(rest, fdiv(lane - 128.0, 32.0), fmod(fdiv(slot, 8.0), 4.0))
+    return (
+        (level == fdiv(g, 40.0)) & (h == fmod(g, 2.0)) & (c == part)
+        & (group == fmod(fdiv(slot, 8.0), 4.0))
+    )
+
+
+def fold(cosine, sine):
+    n = cosine.shape[0] // SLOTS
+    lane = fiota((1, 1, 128), 2)
+    cosine = jnp.reshape(cosine, (n, SLOTS, 128))
+    sine = jnp.reshape(sine, (n, SLOTS, 128))
+    main = jnp.where(lane < 80.0, cosine, sine)
+    rest = jnp.where(lane < 32.0, sine, 0.0)
+    first = rest[:, 0:8]
+    for b in range(1, 4):
+        moved = pltpu.roll(jnp.reshape(rest[:, 8 * b:8 * b + 8], (8 * n, 128)), 32 * b, 1)
+        first = first + jnp.reshape(moved, (n, 8, 128))
+    return main, first, rest[:, 32:40]
+
+
+def unfold(folded):
+    n = folded.shape[0]
+    lane = fiota((1, 1, 128), 2)
+    main = folded[:, 0:40]
+    first = jnp.reshape(folded[:, 40:48], (8 * n, 128))
+    parts = [folded[:, 40:48]]
+    for b in range(1, 4):
+        parts.append(jnp.reshape(pltpu.roll(first, 128 - 32 * b, 1), (n, 8, 128)))
+    parts.append(folded[:, 48:56])
+    rest = jnp.concatenate(parts, axis=1)
+    cosine = jnp.where(lane < 80.0, main, 0.0)
+    sine = jnp.where(lane < 32.0, rest, jnp.where(lane < 80.0, 0.0, main))
+    return jnp.reshape(cosine, (n * SLOTS, 128)), jnp.reshape(sine, (n * SLOTS, 128))
 
 
 def slot_lanes():
@@ -169,10 +202,10 @@
 
 
 def spread_weighted(weighted, selector, spreader):
-    chosen = dot(selector, weighted)
+    chosen = jnp.concatenate([dot(q, weighted) for q in selector], axis=1)
     chosen = jnp.where(level_mask(), chosen, 0.0).astype(BF16)
     wide = dot(chosen, spreader)
-    slot = row_codes()[0]
+    slot = row_codes(fiota((384, 1), 0))[0]
     return jnp.where(slot == slot_lanes(), wide, 0.0).astype(BF16)
 
 
@@ -231,19 +264,20 @@
 
 def collapse(x_even, x_odd, selector_t, spreader):
     both = jnp.concatenate([x_even, x_odd], axis=0)
-    slot = row_codes()[0]
+    slot = row_codes(fiota((384, 1), 0))[0]
     both = jnp.where(slot == slot_lanes(), both, 0.0).astype(BF16)
     rows = dot_nt(both, spreader)
     rows = jnp.where(level_mask(), rows, 0.0).astype(BF16)
-    return dot(selector_t, rows).astype(BF16)
+    folded = dot(selector_t[0], rows[:, 0:128]) + dot(selector_t[1], rows[:, 128:256])
+    return folded.astype(BF16)
 
 
 def kernel(
     level_hbm, wind_hbm, zonal_hbm, weight_hbm, leg_hbm, wave_hbm, damp_hbm, vert_hbm,
     grid_ref, spec_ref,
     native, zonal_ref, weight_ref, leg_ref, wave_ref, damp_ref, vert_ref,
-    field_ref, field_near, column_out, column_in, edge_in, own_block, near_block, wave_col,
-    table_hi, table_lo, near_hi, near_lo, reversed_ref, part_out, part_in, spread_ref,
+    field_ref, field_near, column_out, column_in, edge_in, wave_col,
+    cos_hi, cos_lo, sin_hi, sin_lo, near_cos_hi, near_cos_lo, near_sin_hi, near_sin_lo, reversed_ref, part_out, part_in, spread_ref,
     packed_ref, core_in, sum_out, sum_in, first_ref, gathered, coefs,
     load_sem, edge_send, edge_recv, near_send, near_recv, part_send, part_recv, core_send,
     core_recv, sum_send, sum_recv, all_send, all_recv, pair_send, pair_recv, coef_send,
@@ -338,19 +372,23 @@
     waves = jnp.concatenate(waves, axis=1)
     first_ref[...] = jnp.broadcast_to(first_wave(waves, flon), (64, 128))
 
-    def fill(source, hi, lo, at, first):
-        w = wave_col[pl.ds(pl.multiple_of(source * SLOTS, 8), SLOTS), 0:1]
+    own_tables = (cos_hi, cos_lo, sin_hi, sin_lo)
+    near_tables = (near_cos_hi, near_cos_lo, near_sin_hi, near_sin_lo)
+
+    def fill(source, tables, at, first):
+        w = wave_col[pl.ds(pl.multiple_of(source * SLOTS, 80), 2 * SLOTS), 0:1]
+        rows = pl.ds(pl.multiple_of(at * SLOTS, 80), 2 * SLOTS)
         c, s = trig(w, first)
-        high, low = split(jnp.concatenate([c, s], axis=0))
-        hi[at] = high
-        lo[at] = low
+        tables[0][rows, :], tables[1][rows, :] = split(c)
+        tables[2][rows, :], tables[3][rows, :] = split(s)
 
     near_first = near.astype(F32) * 160.0
 
-    @pl.loop(0, 8)
+    @pl.loop(0, 4)
     def _(zz):
-        fill(x_lo * 8 + zz, table_hi, table_lo, x_lo * 8 + zz, flon * 160.0)
-        fill(x_lo * 8 + zz, near_hi, near_lo, zz, near_first)
+        source = x_lo * 8 + zz * 2
+        fill(source, own_tables, source, flon * 160.0)
+        fill(source, near_tables, zz * 2, near_first)
 
     pl.semaphore_wait(barrier, 3 + 7 + 9)
 
@@ -371,8 +409,6 @@
     zonal = column(zonal_ref[...], picked)
     weight = column(weight_ref[...], picked) * (1.0 / float(NLON) ** 0.5)
     g = fiota((40, 1), 0)
-    own_block[80:128, :] = jnp.zeros((48, LANES), F32)
-    near_block[80:128, :] = jnp.zeros((48, LANES), F32)
     first = first_ref[0:PACK, 0:1]
     sign = parity_sign(first)
     selector, spreader = select_rows(), spread_rows()
@@ -385,30 +421,37 @@
     for step in (2, 6):
         tell(heard.at[1], (y_at(step), lon))
 
-    def advance(block, field, out):
+    def advance(block, field):
+        levels = []
         for l in range(2):
             east = column(column_in[block, 0, 0:1, :], g + 40.0 * l)
             west = column(column_in[block, 1, 0:1, :], g + 40.0 * l)
-            out[40 * l:40 * (l + 1), :] = step_field(
+            levels.append(step_field(
                 field[l], (field[2], field[3]), edge_in[block, 0, l], edge_in[block, 1, l],
                 lat == 0, lat == 31, east, west, zonal, weight, roll,
-            )
-
-    advance(0, field_ref, own_block)
-    advance(1, field_near, near_block)
-
-    def wide(ref):
-        return jnp.reshape(ref[...], (8 * 80, LANES))
-
-    own_hi, own_lo = split(own_block[...])
-    near_h, near_l = split(near_block[...])
-    mine = pl.ds(x_lo * 8, 8)
-    t_hi = jnp.reshape(table_hi[mine], (640, LANES))
-    t_lo = jnp.reshape(table_lo[mine], (640, LANES))
-    n_hi, n_lo = wide(near_hi), wide(near_lo)
-    partial = dot_nt(t_hi, own_hi) + dot_nt(t_hi, own_lo) + dot_nt(t_lo, own_hi)
-    partial = partial + dot_nt(n_hi, near_h) + dot_nt(n_hi, near_l) + dot_nt(n_lo, near_h)
-    part_out[...] = jnp.reshape(partial, (8, 80, 128))
+            ))
+        return jnp.concatenate(levels, axis=0)
+
+    mine = pl.ds(pl.multiple_of(x_lo * 320, 320), 320)
+
+    def fourier(values, tables, rows):
+        zeros = jnp.zeros((48, LANES), F32)
+        sums = []
+        for part, v in enumerate((
+            jnp.concatenate([values, zeros], axis=0),
+            jnp.concatenate([values[48:80], zeros, values[0:48]], axis=0),
+        )):
+            v_hi, v_lo = split(v)
+            t_hi, t_lo = tables[2 * part][rows, :], tables[2 * part + 1][rows, :]
+            sums.append(dot_nt(t_hi, v_hi) + dot_nt(t_hi, v_lo) + dot_nt(t_lo, v_hi))
+        return sums
+
+    own_sums = fourier(advance(0, field_ref), own_tables, mine)
+    near_sums = fourier(advance(1, field_near), near_tables, pl.ds(0, 320))
+    main, rest, rest2 = fold(*(a + b for a, b in zip(own_sums, near_sums)))
+    part_out[:, 0:40, :] = main
+    part_out[:, 40:48, :] = rest
+    part_out[:, 48:56, :] = rest2
 
     def part_copy(o):
         other = z_at(o)
@@ -466,10 +509,10 @@
 
     sum_in[chip] = sum_out[chip]
 
-    @pl.loop(0, 8)
+    @pl.loop(0, 4)
     def _(zz):
-        source = (1 - x_lo) * 8 + zz
-        fill(source, table_hi, table_lo, source, flon * 160.0)
+        source = (1 - x_lo) * 8 + zz * 2
+        fill(source, own_tables, source, flon * 160.0)
 
 
     @pl.loop(1, CHIPS)
@@ -560,11 +603,12 @@
         forward_copy(other).start()
 
     def inverse(half):
-        rows = pl.ds(half * 8, 8)
-        values = jnp.reshape(coefs[rows], (640, 128)).T
-        return dot(values, jnp.reshape(table_hi[rows], (640, LANES))) + dot(
-            values, jnp.reshape(table_lo[rows], (640, LANES))
-        )
+        rows = pl.ds(pl.multiple_of(half * 320, 320), 320)
+        parts = []
+        for part, v in enumerate(unfold(coefs[pl.ds(half * 8, 8)].astype(F32))):
+            v = v.T.astype(BF16)
+            parts.append(dot(v, own_tables[2 * part][rows, :]) + dot(v, own_tables[2 * part + 1][rows, :]))
+        return parts[0][0:80] + jnp.concatenate([parts[1][80:128], parts[1][0:32]], axis=0)
 
     grid = inverse(x_lo)
 
@@ -577,7 +621,7 @@
         ).wait_recv()
 
     grid = grid + inverse(1 - x_lo)
-    grid_ref[...] = grid[0:GRID] * (1.0 / float(NLON * M) ** 0.5)
+    grid_ref[...] = grid * (1.0 / float(NLON * M) ** 0.5)
 
     @pl.loop(1, 8)
     def _(o):
@@ -622,16 +666,18 @@
             pltpu.VMEM((2, 8, 128), F32),
             pltpu.VMEM((2, 2, 8, 128), F32),
             pltpu.VMEM((2, 2, 2, 8, LANES), F32),
-            pltpu.VMEM((128, LANES), F32),
-            pltpu.VMEM((128, LANES), F32),
             pltpu.VMEM((M, 128), F32),
-            pltpu.VMEM((16, 80, LANES), BF16),
-            pltpu.VMEM((16, 80, LANES), BF16),
-            pltpu.VMEM((8, 80, LANES), BF16),
-            pltpu.VMEM((8, 80, LANES), BF16),
+            pltpu.VMEM((M, LANES), BF16),
+            pltpu.VMEM((M, LANES), BF16),
+            pltpu.VMEM((M, LANES), BF16),
+            pltpu.VMEM((M, LANES), BF16),
+            pltpu.VMEM((M // 2, LANES), BF16),
+            pltpu.VMEM((M // 2, LANES), BF16),
+            pltpu.VMEM((M // 2, LANES), BF16),
+            pltpu.VMEM((M // 2, LANES), BF16),
             pltpu.VMEM((K, M), BF16),
-            pltpu.VMEM((8, 80, 128), F32),
-            pltpu.VMEM((8, 80, 128), F32),
+            pltpu.VMEM((8, FOLDED, 128), F32),
+            pltpu.VMEM((8, FOLDED, 128), F32),
             pltpu.VMEM((384, K), BF16),
             pltpu.VMEM((2, BLOCKS, 16, 128), F32),
             pltpu.VMEM((BLOCKS, 16, 128), F32),
@@ -639,7 +685,7 @@
             pltpu.VMEM((CHIPS, 16, 128), F32),
             pltpu.VMEM((64, 128), F32),
             pltpu.VMEM((2, BLOCKS, 16, 128), BF16),
-            pltpu.VMEM((16, 80, 128), BF16),
+            pltpu.VMEM((16, FOLDED16, 128), BF16),
             dma((8,)), dma((8,)), dma((8,)), dma, dma, dma((8,)), dma((8,)), dma, dma,
             dma((CHIPS,)), dma((CHIPS,)), dma((CHIPS,)), dma((CHIPS,)), dma, dma,
             dma((8,)), dma((8,)), dma((8,)), dma((8,)),

time: 63.3 us -> 60.2 us (0.951)
  Pallas kernels: 60.2 us -> 57.1 us
    pallas_call x1, Pallas kernels: 60.2 us -> 57.1 us  [shards(): pl.pallas_call(kernel, out_shape=(jax.ShapeDtypeStruct((GRID, LANES), F32...]
where the time goes in v3:
time: 60.2 us; the launch traced here: 60 us
  Pallas kernels  57.1 us (95%)
  local copies, waits for them, and re-layouts  2.3 us (4%)
  between operations  0.65 us (1%)
    pallas_call x1, Pallas kernels, shards(): pl.pallas_call(kernel, out_shape=(jax.ShapeDtypeStruct((GRID, LANES), F32...  57.1 us
    reshape x1, local copies, waits for them, and re-layouts, shards(): fields = grid[:, :160].reshape(2, ROWS, 2, 160).transpose(0, 2, 1, 3)  1.57 us

profile of v3, /device:TPU:1, one launch (start us, length us, event | category | flops | bytes accessed | tf_op | source)
XLA Modules:
  0.0 60.0 jit_solution(2366892890415832144)
XLA Ops:
  0.6 57.1 %shard_map.95 = (f32[80,256]{1,0:T(8,128)}, f32[32,160]{1,0:T(8,128)}) custom-call(f32[2,20,2,160]{3,2,1,0:T(2,128)} %bitcast.12, f32[2,20,2,160]{3,2,1,0:T(2,128)} %bitcast.13, f32[1,20]{1,0:T(1,128)} %bitcast.18, f32[1,20]{1,0:T(1,128)} %bitcast.19, bf16[800,640]{1,0:T(8,128)(2,1)} %bitcast.11, s32[5,128]{1,0:T(8,128)} %bitcast.17, f32[2]{0:T(128)} %damp_hbm.1, ...), custom_call_target="tpu_custom_call" | custom-call | tf_op jit(solution)/shard_map/pallas_call | solution.py:648
  57.7 0.0 copy-start
  57.7 1.6 %reshape.18 = f32[2,20,2,160]{3,2,1,0:T(2,128)} reshape(f32[80,160]{1,0:T(8,128)} %bitcast.15) | data formatting | bytes 102400 | tf_op jit(solution)/shard_map/reshape | solution.py:701
  59.3 0.0 copy-done
  59.3 0.7 %reshape.19 = f32[20,2,2,40]{3,2,1,0:T(2,128)} reshape(f32[20,160]{1,0:T(8,128)S(1)} %slice.7) | data formatting | bytes 25600 | tf_op jit(solution)/shard_map/reshape | solution.py:702
  (1 shorter events, 0.0 us)
Async XLA Ops:
  57.7 1.6 %copy-start = (f32[32,160]{1,0:T(8,128)S(1)}, f32[32,160]{1,0:T(8,128)}, u32[]{:S(2)}) copy-start(f32[32,160]{1,0:T(8,128)} %get-tuple-element.5) | copy-start | bytes 61444

commit v4 on v3

--- a/solution.py
+++ b/solution.py
@@ -22,8 +22,8 @@
 F32 = jnp.float32
 BF16 = jnp.bfloat16
 MESH = pl.DeviceIdType.MESH
-FAR_FIRST = (12, 11, 13, 4, 10, 14, 3, 5, 9, 15, 8, 2, 6, 1, 7)
-Z_FAR_FIRST = (4, 3, 5, 2, 6, 1, 7)
+FAR_FIRST = (12, 13, 15, 11, 14, 10, 9, 4, 8, 5, 7, 3, 6, 2, 1)
+Z_FAR_FIRST = (4, 5, 7, 3, 6, 2, 1)
 
 
 def fiota(shape, dim):
@@ -276,7 +276,7 @@
     level_hbm, wind_hbm, zonal_hbm, weight_hbm, leg_hbm, wave_hbm, damp_hbm, vert_hbm,
     grid_ref, spec_ref,
     native, zonal_ref, weight_ref, leg_ref, wave_ref, damp_ref, vert_ref,
-    field_ref, field_near, column_out, column_in, edge_in, wave_col,
+    field_ref, tail_out, near_in, column_out, column_in, edge_in, wave_col,
     cos_hi, cos_lo, sin_hi, sin_lo, near_cos_hi, near_cos_lo, near_sin_hi, near_sin_lo, reversed_ref, part_out, part_in, spread_ref,
     packed_ref, core_in, sum_out, sum_in, first_ref, gathered, coefs,
     load_sem, edge_send, edge_recv, near_send, near_recv, part_send, part_recv, core_send,
@@ -296,17 +296,19 @@
     flat = lat.astype(F32)
     flon = lon.astype(F32)
 
-    def chip_at(offset):
-        return (chip // 8 * 8 + offset // 8 * 8) % CHIPS + (chip + offset) % 8
+    def partners(at, bits):
+        flips = [(1 - 2 * ((at // 2**k) % 2)) * 2**k for k in range(bits)]
+        return [at + sum(f for k, f in enumerate(flips) if (o >> k) & 1) for o in range(2**bits)]
+
+    chips = partners(chip, 4)
+    zs = partners(z, 3)
+    lons = [x_lo * 8 + other for other in zs]
 
     def y_at(offset):
         return ((chip // 8) * 8 + (chip + offset) % 8) * 2 + core
 
     def tell(sem, device):
         pl.semaphore_signal(sem, inc=1, device_id=device, device_id_type=MESH)
-
-    def z_at(offset):
-        return (z + offset) % 8
 
     def send(src, dst, send_sem, recv_sem, device):
         copy = pltpu.make_async_remote_copy(
@@ -340,9 +342,8 @@
     for step in (1, 7):
         greet((y_at(step), lon))
 
-    @pl.loop(1, 8)
-    def _(o):
-        greet((lat, x_lo * 8 + z_at(o)))
+    for o in range(1, 8):
+        greet((lat, lons[o]))
 
     edge_devices = (
         ((lat_next, lon), 0, 0), ((lat_prev, lon), 0, 1), ((lat_next, near), 1, 0), ((lat_prev, near), 1, 1),
@@ -362,16 +363,14 @@
             for i in range(ROWS):
                 field_ref[2 * a + b, 2 * i:2 * i + 2, 0:160] = native[a, b, i]
 
+    tail = field_ref[0, :, 128:LANES]
+    for f in range(1, 4):
+        tail = tail + pltpu.roll(field_ref[f, :, 128:LANES], 32 * f, 1)
+    tail_out[...] = tail
+
     flat_level = jnp.reshape(field_ref[0:2], (GRID, LANES))
     column_out[0] = jnp.broadcast_to(as_row(flat_level[:, 0:1]), (8, 128))
     column_out[1] = jnp.broadcast_to(as_row(flat_level[:, 159:160]), (8, 128))
-    waves = wave_ref[...].astype(F32)
-    waves = [waves[t:t + 1, :] for t in range(5)]
-    for t in range(5):
-        wave_col[128 * t:128 * (t + 1), :] = jnp.broadcast_to(waves[t], (128, 128)).T
-    waves = jnp.concatenate(waves, axis=1)
-    first_ref[...] = jnp.broadcast_to(first_wave(waves, flon), (64, 128))
-
     own_tables = (cos_hi, cos_lo, sin_hi, sin_lo)
     near_tables = (near_cos_hi, near_cos_lo, near_sin_hi, near_sin_lo)
 
@@ -384,15 +383,10 @@
 
     near_first = near.astype(F32) * 160.0
 
-    @pl.loop(0, 4)
-    def _(zz):
-        source = x_lo * 8 + zz * 2
-        fill(source, own_tables, source, flon * 160.0)
-        fill(source, near_tables, zz * 2, near_first)
-
     pl.semaphore_wait(barrier, 3 + 7 + 9)
 
-    to_near = send(field_ref, field_near, near_send, near_recv, (lat, near))
+    to_near = send(field_ref.at[:, :, 0:128], near_in.at[0:4], near_send.at[0], near_recv.at[0], (lat, near))
+    to_near2 = send(tail_out, near_in.at[4], near_send.at[1], near_recv.at[1], (lat, near))
     edges = []
     for n, (device, block, side) in enumerate(edge_devices):
         if n < 4:
@@ -405,6 +399,19 @@
     for step in (1, 7):
         tell(heard.at[0], (y_at(step), lon))
 
+    waves = wave_ref[...].astype(F32)
+    waves = [waves[t:t + 1, :] for t in range(5)]
+    for t in range(5):
+        wave_col[128 * t:128 * (t + 1), :] = jnp.broadcast_to(waves[t], (128, 128)).T
+    waves = jnp.concatenate(waves, axis=1)
+    first_ref[...] = jnp.broadcast_to(first_wave(waves, flon), (64, 128))
+
+    @pl.loop(0, 4)
+    def _(zz):
+        source = x_lo * 8 + zz * 2
+        fill(source, own_tables, source, flon * 160.0)
+        fill(source, near_tables, zz * 2, near_first)
+
     picked = fdiv(fiota((40, 1), 0), 2.0)
     zonal = column(zonal_ref[...], picked)
     weight = column(weight_ref[...], picked) * (1.0 / float(NLON) ** 0.5)
@@ -416,6 +423,15 @@
     for copy in edges:
         copy.wait()
     to_near.wait()
+    to_near2.wait()
+    tail = near_in[4]
+    in_tail = fiota((40, 128), 1) < 32.0
+    field_near = [
+        jnp.concatenate(
+            [near_in[f], jnp.where(in_tail, pltpu.roll(tail, (128 - 32 * f) % 128, 1) if f else tail, 0.0)], axis=1
+        )
+        for f in range(4)
+    ]
 
     pl.semaphore_wait(heard.at[0], 2)
     for step in (2, 6):
@@ -453,31 +469,27 @@
     part_out[:, 40:48, :] = rest
     part_out[:, 48:56, :] = rest2
 
+    def remote(src, dst, send_sem, recv_sem, device):
+        return pltpu.make_async_remote_copy(
+            src_ref=src, dst_ref=dst, send_sem=send_sem, recv_sem=recv_sem,
+            device_id=device, device_id_type=MESH,
+        )
+
     def part_copy(o):
-        other = z_at(o)
-        return pltpu.make_async_remote_copy(
-            src_ref=part_out.at[other], dst_ref=part_in.at[z], send_sem=part_send.at[o],
-            recv_sem=part_recv.at[z], device_id=(lat, x_lo * 8 + other), device_id_type=MESH,
-        )
-
+        return remote(part_out.at[zs[o]], part_in.at[o], part_send, part_recv, (lat, lons[o]))
+
+    part_all = remote(part_out.at[0:7], part_in.at[1:8], part_send, part_recv, (lat, lons[1]))
     for o in Z_FAR_FIRST:
         part_copy(o).start()
 
     pl.semaphore_wait(heard.at[1], 2)
     tell(heard.at[2], across)
-    part_in[z] = part_out[z]
+    part_in[0] = part_out[z]
     loads[7].wait()
     leg = leg_ref[...]
     reversed_ref[...] = dot(leg, reverse_matrix()).astype(BF16)
 
-    @pl.loop(1, 8)
-    def _(o):
-        other = z_at(o)
-        pltpu.make_async_remote_copy(
-            src_ref=part_out.at[other], dst_ref=part_in.at[other], send_sem=part_send.at[o],
-            recv_sem=part_recv.at[other], device_id=(lat, x_lo * 8 + other), device_id_type=MESH,
-        ).wait_recv()
-
+    part_all.wait_recv()
     weighted = jnp.sum(part_in[...], axis=0).astype(BF16)
     spread_ref[...] = spread_weighted(weighted, selector, spreader)
     even = dot(spread_ref[0:192], leg)
@@ -497,17 +509,17 @@
     sum_out[...] = packed_ref[core] + core_in[...]
     pl.semaphore_wait(heard.at[2], 1)
 
+    def lat_device(o):
+        return (chips[o] * 2 + core, lon)
+
     def sum_copy(o):
-        other = chip_at(o)
-        return pltpu.make_async_remote_copy(
-            src_ref=sum_out.at[other], dst_ref=sum_in.at[chip], send_sem=sum_send.at[o],
-            recv_sem=sum_recv.at[chip], device_id=(other * 2 + core, lon), device_id_type=MESH,
-        )
-
+        return remote(sum_out.at[chips[o]], sum_in.at[o], sum_send, sum_recv, lat_device(o))
+
+    sum_all = remote(sum_out.at[0:15], sum_in.at[1:16], sum_send, sum_recv, lat_device(1))
     for o in FAR_FIRST:
         sum_copy(o).start()
 
-    sum_in[chip] = sum_out[chip]
+    sum_in[0] = sum_out[chip]
 
     @pl.loop(0, 4)
     def _(zz):
@@ -515,14 +527,7 @@
         fill(source, own_tables, source, flon * 160.0)
 
 
-    @pl.loop(1, CHIPS)
-    def _(o):
-        other = chip_at(o)
-        pltpu.make_async_remote_copy(
-            src_ref=sum_out.at[other], dst_ref=sum_in.at[other], send_sem=sum_send.at[o],
-            recv_sem=sum_recv.at[other], device_id=(other * 2 + core, lon), device_id_type=MESH,
-        ).wait_recv()
-
+    sum_all.wait_recv()
     total = jnp.sum(sum_in[...], axis=0)
     damping = (damp_ref[0], damp_ref[1])
     vertical = ((vert_ref[0, 0], vert_ref[0, 1]), (vert_ref[1, 0], vert_ref[1, 1]))
@@ -531,22 +536,12 @@
     spec = correct(total, first8, lane0, chip == 15, damping, vertical)
     gathered[core, chip] = spec.astype(BF16)
 
-    def all_copy(o):
-        return pltpu.make_async_remote_copy(
-            src_ref=gathered.at[core, chip], dst_ref=gathered.at[core, chip], send_sem=all_send.at[o],
-            recv_sem=all_recv.at[chip], device_id=(chip_at(o) * 2 + core, lon), device_id_type=MESH,
-        )
-
+    mine_all = gathered.at[core, chip]
+    others = gathered.at[core, 0:15]
+    all_all = remote(others, others, all_send, all_recv, lat_device(1))
     for o in FAR_FIRST:
-        all_copy(o).start()
-
-    @pl.loop(1, CHIPS)
-    def _(o):
-        other = chip_at(o)
-        pltpu.make_async_remote_copy(
-            src_ref=gathered.at[core, other], dst_ref=gathered.at[core, other], send_sem=all_send.at[o],
-            recv_sem=all_recv.at[other], device_id=(other * 2 + core, lon), device_id_type=MESH,
-        ).wait_recv()
+        remote(mine_all, mine_all, all_send, all_recv, lat_device(o)).start()
+    all_all.wait_recv()
 
     to_pair = send(gathered.at[core], gathered.at[core], pair_send, pair_recv, (sibling, lon))
     to_pair.wait()
@@ -570,37 +565,23 @@
     x_odd = dot_nt(rows_o, reversed_ref[...])
     coefs[lon] = collapse(x_even, x_odd, select_rows_t(), spreader)
 
-    def coef_copy(o):
-        return pltpu.make_async_remote_copy(
-            src_ref=coefs.at[lon], dst_ref=coefs.at[lon], send_sem=coef_send.at[o],
-            recv_sem=coef_recv.at[z], device_id=(lat, x_lo * 8 + z_at(o)), device_id_type=MESH,
-        )
-
-    def forward_copy(source):
-        at = x_lo * 8 + source
-        return pltpu.make_async_remote_copy(
-            src_ref=coefs.at[at], dst_ref=coefs.at[at], send_sem=fwd_send.at[source],
-            recv_sem=fwd_recv.at[source], device_id=(lat, near), device_id_type=MESH,
-        )
-
-    forward_copy(z).start()
+    def coef_copy(o, at):
+        return remote(coefs.at[at], coefs.at[at], coef_send, coef_recv.at[o], (lat, lons[o]))
+
+    def forward_copy(o):
+        return remote(coefs.at[lons[o]], coefs.at[lons[o]], fwd_send, fwd_recv, (lat, near))
 
     for o in Z_FAR_FIRST:
-        coef_copy(o).start()
+        coef_copy(o, lon).start()
+    forward_copy(0).start()
 
     evens = jnp.concatenate(evens, axis=0).astype(BF16)
     odds = jnp.concatenate(odds, axis=0).astype(BF16)
     spec_ref[...] = spectrum_rows(evens, odds, flat)
 
-    @pl.loop(1, 8)
-    def _(o):
-        other = z_at(o)
-        at = x_lo * 8 + other
-        pltpu.make_async_remote_copy(
-            src_ref=coefs.at[at], dst_ref=coefs.at[at], send_sem=coef_send.at[o],
-            recv_sem=coef_recv.at[other], device_id=(lat, at), device_id_type=MESH,
-        ).wait_recv()
-        forward_copy(other).start()
+    for o in (1, 2, 6, 3, 7, 5, 4):
+        coef_copy(o, lons[o]).wait_recv()
+        forward_copy(o).start()
 
     def inverse(half):
         rows = pl.ds(pl.multiple_of(half * 320, 320), 320)
@@ -612,30 +593,21 @@
 
     grid = inverse(x_lo)
 
-    @pl.loop(0, 8)
-    def _(source):
-        at = (1 - x_lo) * 8 + source
-        pltpu.make_async_remote_copy(
-            src_ref=coefs.at[at], dst_ref=coefs.at[at], send_sem=fwd_send.at[source],
-            recv_sem=fwd_recv.at[source], device_id=(lat, near), device_id_type=MESH,
-        ).wait_recv()
+    forward_all = remote(coefs.at[0:8], coefs.at[0:8], fwd_send, fwd_recv, (lat, near))
+    forward_all.wait_recv()
 
     grid = grid + inverse(1 - x_lo)
-    grid_ref[...] = grid * (1.0 / float(NLON * M) ** 0.5)
-
-    @pl.loop(1, 8)
-    def _(o):
-        part_copy(o).wait_send()
-        coef_copy(o).wait_send()
-
-    @pl.loop(0, 8)
-    def _(source):
-        forward_copy(source).wait_send()
-
-    @pl.loop(1, CHIPS)
-    def _(o):
-        sum_copy(o).wait_send()
-        all_copy(o).wait_send()
+    grid = grid * (1.0 / float(NLON * M) ** 0.5)
+    for l in range(2):
+        for i in range(ROWS):
+            at = 40 * l + 2 * i
+            grid_ref[l, i] = grid[at:at + 2, 0:160]
+
+    part_all.wait_send()
+    sum_all.wait_send()
+    all_all.wait_send()
+    remote(coefs.at[0:7], coefs.at[0:7], coef_send, coef_recv.at[0], (lat, near)).wait_send()
+    forward_all.wait_send()
 
 
 def shards(level_fields, wind_field, zonal_step, quad_weight, legendre, wave_table, damping, vertical):
@@ -648,7 +620,7 @@
     grid, spec = pl.pallas_call(
         kernel,
         out_shape=(
-            jax.ShapeDtypeStruct((GRID, LANES), F32),
+            jax.ShapeDtypeStruct((2, ROWS, 2, 160), F32),
             jax.ShapeDtypeStruct((32, 160), F32),
         ),
         in_specs=[hbm] * 8,
@@ -662,7 +634,8 @@
             pltpu.SMEM((2,), F32),
             pltpu.SMEM((2, 2), F32),
             pltpu.VMEM((4, 40, LANES), F32),
-            pltpu.VMEM((4, 40, LANES), F32),
+            pltpu.VMEM((40, 128), F32),
+            pltpu.VMEM((5, 40, 128), F32),
             pltpu.VMEM((2, 8, 128), F32),
             pltpu.VMEM((2, 2, 8, 128), F32),
             pltpu.VMEM((2, 2, 2, 8, LANES), F32),
@@ -686,10 +659,9 @@
             pltpu.VMEM((64, 128), F32),
             pltpu.VMEM((2, BLOCKS, 16, 128), BF16),
             pltpu.VMEM((16, FOLDED16, 128), BF16),
-            dma((8,)), dma((8,)), dma((8,)), dma, dma, dma((8,)), dma((8,)), dma, dma,
-            dma((CHIPS,)), dma((CHIPS,)), dma((CHIPS,)), dma((CHIPS,)), dma, dma,
-            dma((8,)), dma((8,)), dma((8,)), dma((8,)),
-            pltpu.SemaphoreType.REGULAR((3,)),
+            dma((8,)), dma((8,)), dma((8,)), dma((2,)), dma((2,)), dma, dma, dma,
+            dma, dma, dma, dma, dma, dma, dma, dma,
+            dma((8,)), dma, dma, pltpu.SemaphoreType.REGULAR((3,)),
         ],
         compiler_params=pltpu.CompilerParams(
             collective_id=0, has_side_effects=True, vmem_limit_bytes=60 * 1024 * 1024
@@ -698,7 +670,7 @@
         rows(level_fields), rows(wind_field), zonal_step[None], quad_weight[None],
         legendre.transpose(1, 0, 2).reshape(K, M), wave_table.reshape(5, 128), damping, vertical,
     )
-    fields = grid[:, :160].reshape(2, ROWS, 2, 160).transpose(0, 2, 1, 3)
+    fields = grid.transpose(0, 2, 1, 3)
     spectrum = spec[:ROWS].reshape(ROWS, 2, 2, SLOTS).transpose(0, 3, 1, 2)
     return fields, spectrum
 

time: 60.2 us -> 57.4 us (0.953)
  Pallas kernels: 57.1 us -> 54.5 us
    pallas_call x1, Pallas kernels: 57.1 us -> 54.5 us  [shards(): pl.pallas_call(kernel, out_shape=(jax.ShapeDtypeStruct((2, ROWS, 2, 160),...]
    reshape x1 -> x0, local copies, waits for them, and re-layouts: 1.57 us -> none  [shards(): fields = grid[:, :160].reshape(2, ROWS, 2, 160).transpose(0, 2, 1, 3)]
    slice x1, local copies, waits for them, and re-layouts: 0.01 us -> 0.77 us  [shards(): spectrum = spec[:ROWS].reshape(ROWS, 2, 2, SLOTS).transpose(0, 3, 1, 2)]
    unnamed x2 -> x3, local copies, waits for them, and re-layouts: 0.01 us -> 0.64 us
where the time goes in v4:
time: 57.4 us; the launch traced here: 57.3 us
  Pallas kernels  54.5 us (95%)
  local copies, waits for them, and re-layouts  2.13 us (4%)
  between operations  0.65 us (1%)
    pallas_call x1, Pallas kernels, shards(): pl.pallas_call(kernel, out_shape=(jax.ShapeDtypeStruct((2, ROWS, 2, 160),...  54.5 us

profile of v4, /device:TPU:1, one launch (start us, length us, event | category | flops | bytes accessed | tf_op | source)
XLA Modules:
  0.0 57.3 jit_solution(4340878881725381445)
XLA Ops:
  0.6 54.5 %shard_map.95 = (f32[2,20,2,160]{3,2,1,0:T(2,128)}, f32[32,160]{1,0:T(8,128)}) custom-call(f32[2,20,2,160]{3,2,1,0:T(2,128)} %bitcast.11, f32[2,20,2,160]{3,2,1,0:T(2,128)} %bitcast.12, f32[1,20]{1,0:T(1,128)} %bitcast.16, f32[1,20]{1,0:T(1,128)} %bitcast.17, bf16[800,640]{1,0:T(8,128)(2,1)} %bitcast.10, s32[5,128]{1,0:T(8,128)} %bitcast.15, f32[2]{0:T(128)} %damp_hbm.1, ...), custom_call_target="tpu_custom_call" | custom-call | tf_op jit(solution)/shard_map/pallas_call | solution.py:620
  55.1 0.0 copy-start
  55.1 0.8 %slice.3 = f32[20,160]{1,0:T(8,128)S(1)} slice(f32[32,160]{1,0:T(8,128)} %get-tuple-element.5), slice={[0:20], [0:160]} | slice | bytes 25600 | tf_op jit(solution)/shard_map/slice | solution.py:674
  55.9 0.7 %reshape.15 = f32[20,2,2,40]{3,2,1,0:T(2,128)} reshape(f32[20,160]{1,0:T(8,128)S(1)} %slice.3) | data formatting | bytes 25600 | tf_op jit(solution)/shard_map/reshape | solution.py:674
  56.6 0.0 copy-done
  56.6 0.6 %copy.11 = f32[2,2,20,160]{3,1,2,0:T(2,128)} copy(f32[2,2,20,160]{3,1,2,0:T(2,128)S(1)} %bitcast.13) | data formatting | bytes 102400
Async XLA Ops:
  55.1 1.5 %copy-start = (f32[2,20,2,160]{3,2,1,0:T(2,128)S(1)}, f32[2,20,2,160]{3,2,1,0:T(2,128)}, u32[]{:S(2)}) copy-start(f32[2,20,2,160]{3,2,1,0:T(2,128)} %get-tuple-element.4) | copy-start | bytes 153604

commit v5 on v4

--- a/solution.py
+++ b/solution.py
@@ -385,8 +385,6 @@
 
     pl.semaphore_wait(barrier, 3 + 7 + 9)
 
-    to_near = send(field_ref.at[:, :, 0:128], near_in.at[0:4], near_send.at[0], near_recv.at[0], (lat, near))
-    to_near2 = send(tail_out, near_in.at[4], near_send.at[1], near_recv.at[1], (lat, near))
     edges = []
     for n, (device, block, side) in enumerate(edge_devices):
         if n < 4:
@@ -396,6 +394,8 @@
             src, dst = column_out.at[side], column_in.at[block, side]
         edges.append(send(src, dst, edge_send.at[n], edge_recv.at[n], device))
 
+    to_near = send(field_ref.at[:, :, 0:128], near_in.at[0:4], near_send.at[0], near_recv.at[0], (lat, near))
+    to_near2 = send(tail_out, near_in.at[4], near_send.at[1], near_recv.at[1], (lat, near))
     for step in (1, 7):
         tell(heard.at[0], (y_at(step), lon))
 
@@ -420,8 +420,42 @@
     sign = parity_sign(first)
     selector, spreader = select_rows(), spread_rows()
 
-    for copy in edges:
-        copy.wait()
+    for n in (0, 1, 4, 5):
+        edges[n].wait()
+
+    pl.semaphore_wait(heard.at[0], 2)
+    for step in (2, 6):
+        tell(heard.at[1], (y_at(step), lon))
+
+    def advance(block, field):
+        levels = []
+        for l in range(2):
+            east = column(column_in[block, 0, 0:1, :], g + 40.0 * l)
+            west = column(column_in[block, 1, 0:1, :], g + 40.0 * l)
+            levels.append(step_field(
+                field[l], (field[2], field[3]), edge_in[block, 0, l], edge_in[block, 1, l],
+                lat == 0, lat == 31, east, west, zonal, weight, roll,
+            ))
+        return jnp.concatenate(levels, axis=0)
+
+    mine = pl.ds(pl.multiple_of(x_lo * 320, 320), 320)
+
+    def fourier(values, tables, rows):
+        zeros = jnp.zeros((48, LANES), F32)
+        sums = []
+        for part, v in enumerate((
+            jnp.concatenate([values, zeros], axis=0),
+            jnp.concatenate([values[48:80], zeros, values[0:48]], axis=0),
+        )):
+            v_hi, v_lo = split(v)
+            t_hi, t_lo = tables[2 * part][rows, :], tables[2 * part + 1][rows, :]
+            both = dot_nt(t_hi, jnp.concatenate([v_hi, v_lo], axis=0))
+            sums.append(both[:, 0:128] + both[:, 128:256] + dot_nt(t_lo, v_hi))
+        return sums
+
+    own_sums = fourier(advance(0, field_ref), own_tables, mine)
+    for n in (2, 3, 6, 7):
+        edges[n].wait()
     to_near.wait()
     to_near2.wait()
     tail = near_in[4]
@@ -432,37 +466,6 @@
         )
         for f in range(4)
     ]
-
-    pl.semaphore_wait(heard.at[0], 2)
-    for step in (2, 6):
-        tell(heard.at[1], (y_at(step), lon))
-
-    def advance(block, field):
-        levels = []
-        for l in range(2):
-            east = column(column_in[block, 0, 0:1, :], g + 40.0 * l)
-            west = column(column_in[block, 1, 0:1, :], g + 40.0 * l)
-            levels.append(step_field(
-                field[l], (field[2], field[3]), edge_in[block, 0, l], edge_in[block, 1, l],
-                lat == 0, lat == 31, east, west, zonal, weight, roll,
-            ))
-        return jnp.concatenate(levels, axis=0)
-
-    mine = pl.ds(pl.multiple_of(x_lo * 320, 320), 320)
-
-    def fourier(values, tables, rows):
-        zeros = jnp.zeros((48, LANES), F32)
-        sums = []
-        for part, v in enumerate((
-            jnp.concatenate([values, zeros], axis=0),
-            jnp.concatenate([values[48:80], zeros, values[0:48]], axis=0),
-        )):
-            v_hi, v_lo = split(v)
-            t_hi, t_lo = tables[2 * part][rows, :], tables[2 * part + 1][rows, :]
-            sums.append(dot_nt(t_hi, v_hi) + dot_nt(t_hi, v_lo) + dot_nt(t_lo, v_hi))
-        return sums
-
-    own_sums = fourier(advance(0, field_ref), own_tables, mine)
     near_sums = fourier(advance(1, field_near), near_tables, pl.ds(0, 320))
     main, rest, rest2 = fold(*(a + b for a, b in zip(own_sums, near_sums)))
     part_out[:, 0:40, :] = main

time: 57.4 us -> 56.9 us (level)
  no operation moved by 1% of the time
where the time goes in v5:
time: 56.9 us; the launch traced here: 56.8 us
  Pallas kernels  54 us (95%)
  local copies, waits for them, and re-layouts  2.13 us (4%)
  between operations  0.65 us (1%)
    pallas_call x1, Pallas kernels, shards(): pl.pallas_call(kernel, out_shape=(jax.ShapeDtypeStruct((2, ROWS, 2, 160),...  54 us

profile of v5, /device:TPU:1, one launch (start us, length us, event | category | flops | bytes accessed | tf_op | source)
XLA Modules:
  0.0 56.8 jit_solution(16936033872230139749)
XLA Ops:
  0.6 54.0 %shard_map.95 = (f32[2,20,2,160]{3,2,1,0:T(2,128)}, f32[32,160]{1,0:T(8,128)}) custom-call(f32[2,20,2,160]{3,2,1,0:T(2,128)} %bitcast.11, f32[2,20,2,160]{3,2,1,0:T(2,128)} %bitcast.12, f32[1,20]{1,0:T(1,128)} %bitcast.16, f32[1,20]{1,0:T(1,128)} %bitcast.17, bf16[800,640]{1,0:T(8,128)(2,1)} %bitcast.10, s32[5,128]{1,0:T(8,128)} %bitcast.15, f32[2]{0:T(128)} %damp_hbm.1, ...), custom_call_target="tpu_custom_call" | custom-call | tf_op jit(solution)/shard_map/pallas_call | solution.py:623
  54.6 0.0 copy-start
  54.6 0.8 %slice.3 = f32[20,160]{1,0:T(8,128)S(1)} slice(f32[32,160]{1,0:T(8,128)} %get-tuple-element.5), slice={[0:20], [0:160]} | slice | bytes 25600 | tf_op jit(solution)/shard_map/slice | solution.py:677
  55.4 0.7 %reshape.15 = f32[20,2,2,40]{3,2,1,0:T(2,128)} reshape(f32[20,160]{1,0:T(8,128)S(1)} %slice.3) | data formatting | bytes 25600 | tf_op jit(solution)/shard_map/reshape | solution.py:677
  56.1 0.0 copy-done
  56.1 0.6 %copy.11 = f32[2,2,20,160]{3,1,2,0:T(2,128)} copy(f32[2,2,20,160]{3,1,2,0:T(2,128)S(1)} %bitcast.13) | data formatting | bytes 102400
Async XLA Ops:
  54.6 1.5 %copy-start = (f32[2,20,2,160]{3,2,1,0:T(2,128)S(1)}, f32[2,20,2,160]{3,2,1,0:T(2,128)}, u32[]{:S(2)}) copy-start(f32[2,20,2,160]{3,2,1,0:T(2,128)} %get-tuple-element.4) | copy-start | bytes 153604

commit v6 on v5

--- a/solution.py
+++ b/solution.py
@@ -438,22 +438,29 @@
             ))
         return jnp.concatenate(levels, axis=0)
 
-    mine = pl.ds(pl.multiple_of(x_lo * 320, 320), 320)
-
-    def fourier(values, tables, rows):
+    def parts_of(values):
         zeros = jnp.zeros((48, LANES), F32)
-        sums = []
-        for part, v in enumerate((
+        parts = []
+        for v in (
             jnp.concatenate([values, zeros], axis=0),
             jnp.concatenate([values[48:80], zeros, values[0:48]], axis=0),
-        )):
+        ):
             v_hi, v_lo = split(v)
-            t_hi, t_lo = tables[2 * part][rows, :], tables[2 * part + 1][rows, :]
-            both = dot_nt(t_hi, jnp.concatenate([v_hi, v_lo], axis=0))
-            sums.append(both[:, 0:128] + both[:, 128:256] + dot_nt(t_lo, v_hi))
+            parts.append((jnp.concatenate([v_hi, v_lo], axis=0), v_hi))
+        return parts
+
+    def fourier(parts, tables, first_row):
+        rows = pl.ds(pl.multiple_of(first_row, 32), 160)
+        sums = []
+        for part, (v_both, v_hi) in enumerate(parts):
+            both = dot_nt(tables[2 * part][rows, :], v_both)
+            sums.append(both[:, 0:128] + both[:, 128:256] + dot_nt(tables[2 * part + 1][rows, :], v_hi))
         return sums
 
-    own_sums = fourier(advance(0, field_ref), own_tables, mine)
+    far_half = 1 - z // 4
+    halves = (far_half, 1 - far_half)
+    own_parts = parts_of(advance(0, field_ref))
+    own_sums = [fourier(own_parts, own_tables, x_lo * 320 + half * 160) for half in halves]
     for n in (2, 3, 6, 7):
         edges[n].wait()
     to_near.wait()
@@ -466,12 +473,6 @@
         )
         for f in range(4)
     ]
-    near_sums = fourier(advance(1, field_near), near_tables, pl.ds(0, 320))
-    main, rest, rest2 = fold(*(a + b for a, b in zip(own_sums, near_sums)))
-    part_out[:, 0:40, :] = main
-    part_out[:, 40:48, :] = rest
-    part_out[:, 48:56, :] = rest2
-
     def remote(src, dst, send_sem, recv_sem, device):
         return pltpu.make_async_remote_copy(
             src_ref=src, dst_ref=dst, send_sem=send_sem, recv_sem=recv_sem,
@@ -482,8 +483,17 @@
         return remote(part_out.at[zs[o]], part_in.at[o], part_send, part_recv, (lat, lons[o]))
 
     part_all = remote(part_out.at[0:7], part_in.at[1:8], part_send, part_recv, (lat, lons[1]))
-    for o in Z_FAR_FIRST:
-        part_copy(o).start()
+    near_parts = parts_of(advance(1, field_near))
+    for n, half in enumerate(halves):
+        near_sums = fourier(near_parts, near_tables, half * 160)
+        main, rest, rest2 = fold(*(a + b for a, b in zip(own_sums[n], near_sums)))
+        block = pl.ds(half * 4, 4)
+        part_out[block, 0:40, :] = main
+        part_out[block, 40:48, :] = rest
+        part_out[block, 48:56, :] = rest2
+        for o in Z_FAR_FIRST:
+            if (o >= 4) == (n == 0):
+                part_copy(o).start()
 
     pl.semaphore_wait(heard.at[1], 2)
     tell(heard.at[2], across)
@@ -507,10 +517,10 @@
             rest = jnp.where(lane128 == float(kb), extra[16 * kb:16 * (kb + 1)], rest)
         packed_ref[c, 15] = rest
 
+    pl.semaphore_wait(heard.at[2], 1)
     to_core = send(packed_ref.at[1 - core], core_in, core_send, core_recv, (sibling, lon))
     to_core.wait()
     sum_out[...] = packed_ref[core] + core_in[...]
-    pl.semaphore_wait(heard.at[2], 1)
 
     def lat_device(o):
         return (chips[o] * 2 + core, lon)
@@ -542,12 +552,13 @@
     mine_all = gathered.at[core, chip]
     others = gathered.at[core, 0:15]
     all_all = remote(others, others, all_send, all_recv, lat_device(1))
-    for o in FAR_FIRST:
-        remote(mine_all, mine_all, all_send, all_recv, lat_device(o)).start()
+    both_all = remote(gathered.at[1 - core], gathered.at[1 - core], pair_send, pair_recv, (sibling, lon))
+    for o in FAR_FIRST + (0,):
+        if o:
+            remote(mine_all, mine_all, all_send, all_recv, lat_device(o)).start()
+        remote(mine_all, mine_all, pair_send, pair_recv, (chips[o] * 2 + 1 - core, lon)).start()
     all_all.wait_recv()
-
-    to_pair = send(gathered.at[core], gathered.at[core], pair_send, pair_recv, (sibling, lon))
-    to_pair.wait()
+    both_all.wait_recv()
 
     evens, odds = [], []
     for c in range(2):
@@ -609,6 +620,7 @@
     part_all.wait_send()
     sum_all.wait_send()
     all_all.wait_send()
+    both_all.wait_send()
     remote(coefs.at[0:7], coefs.at[0:7], coef_send, coef_recv.at[0], (lat, near)).wait_send()
     forward_all.wait_send()
 

time: 56.9 us -> 56 us (0.984)
  Pallas kernels: 54 us -> 53 us
    pallas_call x1, Pallas kernels: 54 us -> 53 us  [shards(): pl.pallas_call(kernel, out_shape=(jax.ShapeDtypeStruct((2, ROWS, 2, 160),...]
where the time goes in v6:
time: 56 us; the launch traced here: 55.8 us
  Pallas kernels  53 us (95%)
  local copies, waits for them, and re-layouts  2.13 us (4%)
  between operations  0.65 us (1%)
    pallas_call x1, Pallas kernels, shards(): pl.pallas_call(kernel, out_shape=(jax.ShapeDtypeStruct((2, ROWS, 2, 160),...  53 us

profile of v6, /device:TPU:1, one launch (start us, length us, event | category | flops | bytes accessed | tf_op | source)
XLA Modules:
  0.0 55.8 jit_solution(15409043407864388267)
XLA Ops:
  0.6 53.0 %shard_map.95 = (f32[2,20,2,160]{3,2,1,0:T(2,128)}, f32[32,160]{1,0:T(8,128)}) custom-call(f32[2,20,2,160]{3,2,1,0:T(2,128)} %bitcast.11, f32[2,20,2,160]{3,2,1,0:T(2,128)} %bitcast.12, f32[1,20]{1,0:T(1,128)} %bitcast.16, f32[1,20]{1,0:T(1,128)} %bitcast.17, bf16[800,640]{1,0:T(8,128)(2,1)} %bitcast.10, s32[5,128]{1,0:T(8,128)} %bitcast.15, f32[2]{0:T(128)} %damp_hbm.1, ...), custom_call_target="tpu_custom_call" | custom-call | tf_op jit(solution)/shard_map/pallas_call | solution.py:635
  53.7 0.0 copy-start
  53.7 0.8 %slice.3 = f32[20,160]{1,0:T(8,128)S(1)} slice(f32[32,160]{1,0:T(8,128)} %get-tuple-element.5), slice={[0:20], [0:160]} | slice | bytes 25600 | tf_op jit(solution)/shard_map/slice | solution.py:689
  54.5 0.7 %reshape.15 = f32[20,2,2,40]{3,2,1,0:T(2,128)} reshape(f32[20,160]{1,0:T(8,128)S(1)} %slice.3) | data formatting | bytes 25600 | tf_op jit(solution)/shard_map/reshape | solution.py:689
  55.2 0.0 copy-done
  55.2 0.6 %copy.11 = f32[2,2,20,160]{3,1,2,0:T(2,128)} copy(f32[2,2,20,160]{3,1,2,0:T(2,128)S(1)} %bitcast.13) | data formatting | bytes 102400
Async XLA Ops:
  53.7 1.5 %copy-start = (f32[2,20,2,160]{3,2,1,0:T(2,128)S(1)}, f32[2,20,2,160]{3,2,1,0:T(2,128)}, u32[]{:S(2)}) copy-start(f32[2,20,2,160]{3,2,1,0:T(2,128)} %get-tuple-element.4) | copy-start | bytes 153604

commit v7 on v6

--- a/solution.py
+++ b/solution.py
@@ -354,7 +354,7 @@
         greet(device)
     greet((lat, near))
 
-    for copy in loads[:7]:
+    for copy in loads[:2]:
         copy.wait()
 
     field_ref[:, :, 128:LANES] = jnp.zeros((4, 40, 128), F32)
@@ -399,6 +399,8 @@
     for step in (1, 7):
         tell(heard.at[0], (y_at(step), lon))
 
+    for copy in loads[2:7]:
+        copy.wait()
     waves = wave_ref[...].astype(F32)
     waves = [waves[t:t + 1, :] for t in range(5)]
     for t in range(5):
@@ -410,7 +412,6 @@
     def _(zz):
         source = x_lo * 8 + zz * 2
         fill(source, own_tables, source, flon * 160.0)
-        fill(source, near_tables, zz * 2, near_first)
 
     picked = fdiv(fiota((40, 1), 0), 2.0)
     zonal = column(zonal_ref[...], picked)
@@ -461,6 +462,11 @@
     halves = (far_half, 1 - far_half)
     own_parts = parts_of(advance(0, field_ref))
     own_sums = [fourier(own_parts, own_tables, x_lo * 320 + half * 160) for half in halves]
+
+    @pl.loop(0, 4)
+    def _(zz):
+        fill(x_lo * 8 + zz * 2, near_tables, zz * 2, near_first)
+
     for n in (2, 3, 6, 7):
         edges[n].wait()
     to_near.wait()

time: 56 us -> 56.4 us (level)
  no operation moved by 1% of the time
where the time goes in v7:
time: 56.4 us; the launch traced here: 56.2 us
  Pallas kernels  53.4 us (95%)
  local copies, waits for them, and re-layouts  2.13 us (4%)
  between operations  0.65 us (1%)
    pallas_call x1, Pallas kernels, shards(): pl.pallas_call(kernel, out_shape=(jax.ShapeDtypeStruct((2, ROWS, 2, 160),...  53.4 us

profile of v7, /device:TPU:1, one launch (start us, length us, event | category | flops | bytes accessed | tf_op | source)
XLA Modules:
  0.0 56.2 jit_solution(8837856759892627454)
XLA Ops:
  0.6 53.4 %shard_map.95 = (f32[2,20,2,160]{3,2,1,0:T(2,128)}, f32[32,160]{1,0:T(8,128)}) custom-call(f32[2,20,2,160]{3,2,1,0:T(2,128)} %bitcast.11, f32[2,20,2,160]{3,2,1,0:T(2,128)} %bitcast.12, f32[1,20]{1,0:T(1,128)} %bitcast.16, f32[1,20]{1,0:T(1,128)} %bitcast.17, bf16[800,640]{1,0:T(8,128)(2,1)} %bitcast.10, s32[5,128]{1,0:T(8,128)} %bitcast.15, f32[2]{0:T(128)} %damp_hbm.1, ...), custom_call_target="tpu_custom_call" | custom-call | tf_op jit(solution)/shard_map/pallas_call | solution.py:641
  54.1 0.0 copy-start
  54.1 0.8 %slice.3 = f32[20,160]{1,0:T(8,128)S(1)} slice(f32[32,160]{1,0:T(8,128)} %get-tuple-element.5), slice={[0:20], [0:160]} | slice | bytes 25600 | tf_op jit(solution)/shard_map/slice | solution.py:695
  54.8 0.7 %reshape.15 = f32[20,2,2,40]{3,2,1,0:T(2,128)} reshape(f32[20,160]{1,0:T(8,128)S(1)} %slice.3) | data formatting | bytes 25600 | tf_op jit(solution)/shard_map/reshape | solution.py:695
  55.6 0.0 copy-done
  55.6 0.6 %copy.11 = f32[2,2,20,160]{3,1,2,0:T(2,128)} copy(f32[2,2,20,160]{3,1,2,0:T(2,128)S(1)} %bitcast.13) | data formatting | bytes 102400
Async XLA Ops:
  54.1 1.5 %copy-start = (f32[2,20,2,160]{3,2,1,0:T(2,128)S(1)}, f32[2,20,2,160]{3,2,1,0:T(2,128)}, u32[]{:S(2)}) copy-start(f32[2,20,2,160]{3,2,1,0:T(2,128)} %get-tuple-element.4) | copy-start | bytes 153604
